TPU v7x, 256 devices: a whole 4x4x8 slice. The times are simulated.
256 devices in a mesh: row: 16 (over x, y), col: 16 (over z, core).
Axes of the slice: x: 4, y: 4, z: 8, core: 2. Of those that a mesh axis runs over, the one named last changes fastest.
Arguments:
- matrix: float32 [16384, 8192], P('row', 'col'), may hold values from -3 to 4, as said below
- pattern: int32 [2, 128], replicated, may hold values from 0 to 1, as said below
Outputs:
- panel: float32 [16384, 1024], P('row')
- schur: float32 [16384, 8192], P('row', 'col')
Inputs may be any that keep to these rules, and one draw needn't show every extreme that they name: `matrix`: the leading square of order 2 * 4 * 128 in natural order is symmetric and each diagonal entry exceeds the sum of the magnitudes of the other entries of its row. pattern[1, g] is 1 wherever pattern[0, g] is 1; both are 1 for g below 8.
All inputs are finite; a program needn't handle non-finite values.
Results may differ from a plain program's by a relative error of at most 0.000057.
Values sent between devices are 32-bit elements; how exact they have to be, the bound alone decides.
No kernel may reach another device: no remote copies, remote signals or barrier semaphores. Data moves between devices by JAX's collectives and lax.ppermute only.
A program may use at most 128 MiB of HBM per device.

v0:
```python
import jax
import jax.numpy as jnp
from jax import lax
from jax.sharding import PartitionSpec as P

BLK = 128
PB = 4


precise = lax.Precision.HIGHEST


def spread(x, axis, root):
    mine = lax.axis_index(axis) == root
    return lax.psum(jnp.where(mine, x, jnp.zeros_like(x)), axis)


def factor_diag(diagonal_block, half_width):
    identity = jnp.eye(half_width, dtype=jnp.float32)
    leading = jnp.linalg.cholesky(diagonal_block[:half_width, :half_width])
    leading_inv = jax.scipy.linalg.solve_triangular(leading, identity, lower=True)
    lower_left = jnp.dot(diagonal_block[half_width:, :half_width], leading_inv.T, precision=precise)
    reduced = diagonal_block[half_width:, half_width:] - jnp.dot(
        lower_left, lower_left.T, precision=precise
    )
    second = jnp.linalg.cholesky(reduced)
    second_inv = jax.scipy.linalg.solve_triangular(second, identity, lower=True)
    corner = -jnp.dot(
        second_inv, jnp.dot(lower_left, leading_inv, precision=precise), precision=precise
    )
    zero_block = jnp.zeros((half_width, half_width), jnp.float32)
    factor = jnp.block([[leading, zero_block], [lower_left, second]])
    inverse = jnp.block([[leading_inv, zero_block], [corner, second_inv]])
    return (factor, inverse)


def on_device(matrix, pattern):
    row_count = lax.axis_size("row")
    col_count = lax.axis_size("col")
    row_index = lax.axis_index("row")
    col_index = lax.axis_index("col")
    panel_width = 2 * PB * BLK
    half_width = PB * BLK
    local_rows = matrix.shape[0]
    row_blocks = local_rows // BLK
    col_blocks = matrix.shape[1] // BLK
    groups = (2 * PB + row_count - 1) // row_count
    corner_piece = matrix[: groups * BLK, :BLK]
    top_rows = lax.all_gather(corner_piece, "col", axis=1, tiled=True)[:, :panel_width]
    stacked = lax.all_gather(top_rows, "row", axis=0, tiled=True)
    diagonal_block = stacked.reshape(row_count, groups, BLK, panel_width).transpose(1, 0, 2, 3)
    diagonal_block = diagonal_block.reshape(row_count * groups * BLK, panel_width)[:panel_width]
    factor, inverse = factor_diag(diagonal_block, half_width)
    pattern_grid = pattern.reshape(2, row_blocks, row_count)
    own_pattern = lax.dynamic_index_in_dim(pattern_grid, row_index, axis=2, keepdims=False).astype(
        jnp.float32
    )
    first_mask = jnp.repeat(own_pattern[0], BLK)
    second_mask = jnp.repeat(own_pattern[1], BLK)
    block_ids = jnp.arange(row_blocks, dtype=jnp.int32) * row_count + row_index
    panel_cols = lax.all_gather(matrix[:, :BLK], "col", axis=1, tiled=True)[:, :panel_width]
    masked = jnp.concatenate(
        [
            panel_cols[:, :half_width] * first_mask[:, None],
            panel_cols[:, half_width:] * second_mask[:, None],
        ],
        axis=1,
    )
    solved = jnp.einsum("rk,wk->rw", masked, inverse, precision=precise)
    selector = (block_ids[:, None] == jnp.arange(2 * PB, dtype=jnp.int32)[None, :]).astype(
        jnp.float32
    )
    factor_blocks = factor.reshape(2 * PB, BLK, panel_width)
    placed = jnp.einsum("kp,pbw->kbw", selector, factor_blocks, precision=precise).reshape(
        local_rows, panel_width
    )
    top_flag = jnp.repeat(block_ids < 2 * PB, BLK)
    panel = jnp.where(top_flag[:, None], placed, solved)
    col_per_row = col_count // row_count
    source_row = col_index % row_count
    offset = col_index // row_count
    grouped = panel.reshape(row_blocks // col_per_row, col_per_row, BLK, panel_width)
    chosen = lax.dynamic_index_in_dim(grouped, offset, axis=1, keepdims=False)
    partner = spread(chosen[:col_blocks].reshape(col_blocks * BLK, panel_width), "row", source_row)
    update = jnp.einsum("rw,cw->rc", panel, partner, precision=precise)
    col_ids = jnp.arange(col_blocks, dtype=jnp.int32) * col_count + col_index
    keep_mask = jnp.logical_not(top_flag)[:, None] & jnp.repeat(col_ids >= 2 * PB, BLK)[None, :]
    schur = jnp.where(keep_mask, matrix - update, jnp.zeros_like(update))
    return (panel, schur)


def solution(mesh):
    in_specs = (P("row", "col"), P())
    out_specs = (P("row", None), P("row", "col"))
    return jax.shard_map(
        on_device, mesh=mesh, in_specs=in_specs, out_specs=out_specs, check_vma=False
    )
```

profile of v0, /device:TPU:1, one launch (start us, length us, event | category | flops | bytes accessed | tf_op | source)
XLA Modules:
  0.0 653.5 jit_solution(12977933820273369857)
XLA Ops:
  10.8 42.4 %all-gather.4.cloned.1.call-done = f32[128,2048]{0,1:T(8,128)} async-done(((f32[128,128]{0,1:T(8,128)}), f32[128,2048]{0,1:T(8,128)}) %all-gather.4.cloned.1.call-update) | async-done | bytes 1048592 | tf_op jit(solution)/shard_map/all_gather | solution.py:49
  56.4 64.0 %all-gather.8.cloned.1.call-done = f32[1024,2048]{1,0:T(8,128)} async-done(((f32[1024,128]{1,0:T(8,128)}), f32[1024,2048]{1,0:T(8,128)}) %all-gather.8.cloned.1.call-update) | async-done | bytes 8388624 | tf_op jit(solution)/shard_map/all_gather | solution.py:61
  120.4 4.6 slice_multiply_fusion.1
  125.0 76.5 %all-gather.6.cloned.1.call-done = f32[2048,1024]{0,1:T(8,128)} async-done(((f32[128,1024]{0,1:T(8,128)}), f32[2048,1024]{0,1:T(8,128)}) %all-gather.6.cloned.1.call-update) | async-done | bytes 8388624 | tf_op jit(solution)/shard_map/all_gather | solution.py:50
  204.6 11.7 %cholesky.286 = f32[128,128]{1,0:T(8,128)S(1)} custom-call(f32[128,128]{1,0:T(8,128)S(1)} %cholesky.426), custom_call_target="Cholesky" | custom-call | tf_op jit(solution)/shard_map/jit(cholesky)/cholesky | solution.py:20
  216.3 9.8 %custom-call.27 = f32[1,128,128]{1,2,0:T(8,128)S(1)} custom-call(f32[1,128,128]{2,1,0:T(8,128)S(1)} %get-tuple-element.65), custom_call_target="InvertDiagBlocksLowerTriangular" | custom-call | tf_op jit(solution)/shard_map/jit(cholesky)/cholesky | solution.py:20
  226.9 11.7 %cholesky.305 = f32[128,128]{1,0:T(8,128)S(1)} custom-call(f32[128,128]{1,0:T(8,128)S(1)} %cholesky.430), custom_call_target="Cholesky" | custom-call | tf_op jit(solution)/shard_map/jit(cholesky)/cholesky | solution.py:20
  238.7 10.2 %custom-call.28 = f32[1,128,128]{1,2,0:T(8,128)S(1)} custom-call(f32[1,128,128]{2,1,0:T(8,128)S(1)} %get-tuple-element.62), custom_call_target="InvertDiagBlocksLowerTriangular" | custom-call | tf_op jit(solution)/shard_map/jit(cholesky)/cholesky | solution.py:20
  249.6 11.7 %cholesky.326 = f32[128,128]{1,0:T(8,128)S(1)} custom-call(f32[128,128]{1,0:T(8,128)S(1)} %cholesky.435), custom_call_target="Cholesky" | custom-call | tf_op jit(solution)/shard_map/jit(cholesky)/cholesky | solution.py:20
  261.9 9.8 %custom-call.29 = f32[1,128,128]{1,2,0:T(8,128)S(1)} custom-call(f32[1,128,128]{2,1,0:T(8,128)S(1)} %get-tuple-element.59), custom_call_target="InvertDiagBlocksLowerTriangular" | custom-call | tf_op jit(solution)/shard_map/jit(cholesky)/cholesky | solution.py:20
  272.3 11.9 %cholesky.343 = f32[128,128]{1,0:T(8,128)S(1)} custom-call(f32[128,128]{1,0:T(8,128)S(1)} %convolution_subtract_fusion.12), custom_call_target="Cholesky" | custom-call | tf_op jit(solution)/shard_map/jit(cholesky)/cholesky | solution.py:20
  289.3 8.3 %while.4 = (s32[]{:T(128)}, f32[512,512]{1,0:T(8,128)S(1)}, s32[4,2]{0,1:T(2,128)S(1)}, f32[4,128,128]{2,1,0:T(8,128)S(1)}, s32[]{:T(128)}) while((s32[]{:T(128)}, f32[512,512]{1,0:T(8,128)S(1)}, s32[4,2]{0,1:T(2,128)S(1)}, f32[4,128,128]{2,1,0:T(8,128)S(1)}, s32[]{:T(128)}) %tuple.59), condition=%wide.while_cond, body=%wide.while_body.sunk | while | flops 2 | bytes 131181 | solution.py:21
  297.6 39.3 %custom-call.30 = f32[4,128,128]{1,2,0:T(8,128)S(1)} custom-call(f32[4,128,128]{2,1,0:T(8,128)S(1)} %get-tuple-element.18), custom_call_target="InvertDiagBlocksLowerTriangular" | custom-call | tf_op jit(solution)/shard_map/jit(_solve_triangular)/triangular_solve | solution.py:21
  340.1 3.2 fusion.20
  343.3 2.8 fusion.99
  346.2 3.1 convolution_subtract_fusion
  353.1 12.1 %cholesky.358 = f32[128,128]{1,0:T(8,128)S(1)} custom-call(f32[128,128]{1,0:T(8,128)S(1)} %cholesky.439), custom_call_target="Cholesky" | custom-call | tf_op jit(solution)/shard_map/jit(cholesky)/cholesky | solution.py:26
  365.2 9.8 %custom-call.31 = f32[1,128,128]{1,2,0:T(8,128)S(1)} custom-call(f32[1,128,128]{2,1,0:T(8,128)S(1)} %get-tuple-element.55), custom_call_target="InvertDiagBlocksLowerTriangular" | custom-call | tf_op jit(solution)/shard_map/jit(cholesky)/cholesky | solution.py:26
  379.3 2.2 pad_maximum_fusion
  381.9 11.7 %cholesky.377 = f32[128,128]{1,0:T(8,128)S(1)} custom-call(f32[128,128]{1,0:T(8,128)S(1)} %slice-done), custom_call_target="Cholesky" | custom-call | tf_op jit(solution)/shard_map/jit(cholesky)/cholesky | solution.py:26
  396.0 9.8 %custom-call.32 = f32[1,128,128]{1,2,0:T(8,128)S(1)} custom-call(f32[1,128,128]{2,1,0:T(8,128)S(1)} %get-tuple-element.52), custom_call_target="InvertDiagBlocksLowerTriangular" | custom-call | tf_op jit(solution)/shard_map/jit(cholesky)/cholesky | solution.py:26
  408.2 11.9 %cholesky.398 = f32[128,128]{1,0:T(8,128)S(1)} custom-call(f32[128,128]{1,0:T(8,128)S(1)} %cholesky.448), custom_call_target="Cholesky" | custom-call | tf_op jit(solution)/shard_map/jit(cholesky)/cholesky | solution.py:26
  420.8 9.8 %custom-call.33 = f32[1,128,128]{1,2,0:T(8,128)S(1)} custom-call(f32[1,128,128]{2,1,0:T(8,128)S(1)} %get-tuple-element.49), custom_call_target="InvertDiagBlocksLowerTriangular" | custom-call | tf_op jit(solution)/shard_map/jit(cholesky)/cholesky | solution.py:26
  432.1 11.7 %cholesky.415 = f32[128,128]{1,0:T(8,128)S(1)} custom-call(f32[128,128]{1,0:T(8,128)S(1)} %convolution_subtract_fusion.11), custom_call_target="Cholesky" | custom-call | tf_op jit(solution)/shard_map/jit(cholesky)/cholesky | solution.py:26
  448.6 11.1 %while.5 = (s32[]{:T(128)}, f32[512,512]{1,0:T(8,128)}, s32[4,2]{0,1:T(2,128)S(1)}, f32[4,128,128]{2,1,0:T(8,128)S(1)}, s32[]{:T(128)}) while((s32[]{:T(128)}, f32[512,512]{1,0:T(8,128)}, s32[4,2]{0,1:T(2,128)S(1)}, f32[4,128,128]{2,1,0:T(8,128)S(1)}, s32[]{:T(128)}) %tuple.73), condition=%wide.while_cond.clone, body=%wide.while_body.clone.sunk | while | flops 2 | bytes 131181 | solution.py:27
  449.2 2.2 bitcast_dynamic-update-slice_fusion.5
  460.4 40.3 %custom-call.34 = f32[4,128,128]{1,2,0:T(8,128)S(1)} custom-call(f32[4,128,128]{2,1,0:T(8,128)} %copy-done.13), custom_call_target="InvertDiagBlocksLowerTriangular" | custom-call | tf_op jit(solution)/shard_map/jit(_solve_triangular)/triangular_solve | solution.py:27
  509.8 4.3 fusion.14
  514.2 2.4 copy.23
  518.5 14.6 %bitcast_select_fusion = f32[1024,1024]{1,0:T(8,128)S(1)} fusion(f32[8,128,1024]{2,1,0:T(8,128)S(1)} %copy.23, pred[1024]{0:T(1024)(128)(4,1)S(1)} %broadcast_bitcast_fusion.2, f32[512,512]{1,0:T(8,128)S(1)} %copy-done.11, f32[128,512]{1,0:T(8,128)S(1)} %fusion.70, f32[128,512]{1,0:T(8,128)S(1)} %fusion.71, f32[128,512]{1,0:T(8,128)S(1)} %fusion.73, ...), kind=kOutput, calls=%fused_computation.21 | convolution fusion | flops 12894339072 | bytes 15729664 | tf_op jit(solution)/shard_map/rk,wk->rw/dot_general | solution.py:69
  536.8 99.5 %all-reduce.5.cloned.1.call-done = f32[512,1024]{1,0:T(8,128)} async-done(((f32[512,1024]{1,0:T(8,128)}), f32[512,1024]{1,0:T(8,128)}) %all-reduce.5.cloned.1.call-update) | async-done | bytes 2097168 | tf_op jit(solution)/shard_map/psum | solution.py:15
  636.4 10.4 %subtract_select_fusion = f32[1024,512]{1,0:T(8,128)} fusion(f32[1024,512]{1,0:T(8,128)S(1)} %copy-done.7, f32[1024,1024]{1,0:T(8,128)} %copy-done, f32[512,1024]{1,0:T(8,128)} %all-reduce.5.cloned.1.call-done, pred[512]{0:T(512)(128)(4,1)S(1)} %broadcast_bitcast_fusion.3, pred[1024]{0:T(1024)(128)(4,1)S(1)} %bitcast_not_fusion), kind=kOutput, calls=%fused_computation.29 | convolution fusion | flops 6444023808 | bytes 10487296 | tf_op jit(solution)/shard_map/rw,cw->rc/dot_general | solution.py:85
  (147 shorter events, 68.4 us)
Async XLA Ops:
  7.2 46.1 %all-gather.4.cloned.1.call-start = ((), (), s32[]{:S(2)}) async-start(), calls=%async_computation | async-start | bytes 1114112 | tf_op jit(solution)/shard_map/all_gather | solution.py:49
  8.8 111.6 %all-gather.8.cloned.1.call-start = ((), (), s32[]{:S(2)}) async-start(), calls=%async_computation.2 | async-start | bytes 8912896 | tf_op jit(solution)/shard_map/all_gather | solution.py:61
  10.8 190.7 %all-gather.6.cloned.1.call-start = ((), (), s32[]{:S(2)}) async-start(), calls=%async_computation.1 | async-start | bytes 8912896 | tf_op jit(solution)/shard_map/all_gather | solution.py:50
  55.1 581.3 %all-reduce.5.cloned.1.call-start = ((), (), s32[]{:S(2)}) async-start(), calls=%async_computation.3 | async-start | bytes 4194304 | tf_op jit(solution)/shard_map/psum | solution.py:15
  56.1 68.9 %copy-start.14 = (pred[8]{0:T(512)(128)(4,1)}, pred[8]{0:T(512)(128)(4,1)S(1)}, u32[]{:S(2)}) copy-start(pred[8]{0:T(512)(128)(4,1)S(1)} %broadcast_compare_fusion) | copy-start | bytes 28
  338.2 8.0 %copy-start.1 = (f32[128,512]{1,0:T(8,128)}, f32[128,512]{1,0:T(8,128)S(1)}, u32[]{:S(2)}) copy-start(f32[128,512]{1,0:T(8,128)S(1)} %fusion.79) | copy-start | bytes 786436
  339.0 7.1 %copy-start.2 = (f32[128,512]{1,0:T(8,128)}, f32[128,512]{1,0:T(8,128)S(1)}, u32[]{:S(2)}) copy-start(f32[128,512]{1,0:T(8,128)S(1)} %fusion.77) | copy-start | bytes 786436
  340.1 3.2 copy-start.6
  352.0 1.0 copy-start.8
  379.3 2.7 slice-start
  448.6 60.8 %copy-start.4 = (f32[512,512]{1,0:T(8,128)S(1)}, f32[512,512]{1,0:T(8,128)}, u32[]{:S(2)}) copy-start(f32[512,512]{1,0:T(8,128)} %get-tuple-element.39) | copy-start | bytes 3145732
  459.6 0.7 copy-start.13
  500.7 0.7 copy-start.12
  500.7 8.6 %copy-start.5 = (f32[512,512]{1,0:T(8,128)S(1)}, f32[512,512]{1,0:T(8,128)}, u32[]{:S(2)}) copy-start(f32[512,512]{1,0:T(8,128)} %get-tuple-element.37) | copy-start | bytes 3145732
  514.1 2.5 copy-start.3
  514.1 4.3 copy-start.9
  514.1 4.3 copy-start.10
  514.2 4.3 copy-start.11
  533.1 2.0 copy-start
  535.2 1.6 copy-start.15
  535.2 101.2 %copy-start.7 = (f32[1024,512]{1,0:T(8,128)S(1)}, f32[1024,512]{1,0:T(8,128)}, u32[]{:S(2)}) copy-start(f32[1024,512]{1,0:T(8,128)} %param.5) | copy-start | bytes 6291460
Sparse Core Ops, SparseCore 0:
  10.4 42.7 all-gather.3
  55.5 64.8 all-gather.7
  122.8 78.5 all-gather.5
  536.8 99.5 all-reduce.4
where the time goes:
time: 663 us; the launch traced here: 653 us
  waiting for transfers between devices  282 us (43%)
  other arithmetic  253 us (38%)
  matrix products  60.8 us (9%)
  local copies, waits for them, and re-layouts  37.5 us (6%)
  between operations  19.4 us (3%)
    psum x1, waiting for transfers between devices, spread(): return lax.psum(jnp.where(mine, x, jnp.zeros_like(x)), axis)  99.5 us
    another operation x15, other arithmetic, factor_diag(): second = jnp.linalg.cholesky(reduced)  79.6 us
    another operation x14, other arithmetic, factor_diag(): leading = jnp.linalg.cholesky(diagonal_block[:half_width, :half_width])  78.9 us
    all_gather x1, waiting for transfers between devices, on_device(): stacked = lax.all_gather(top_rows, 'row', axis=0, tiled=True)  76.5 us
    all_gather x1, waiting for transfers between devices, on_device(): lax.all_gather(matrix[:, :BLK], 'col', axis=1, tiled=True)[:, :panel_width]  64 us
    another operation x4, other arithmetic, factor_diag(): jax.scipy.linalg.solve_triangular(leading, identity, lower=True)  42.9 us
    all_gather x1, waiting for transfers between devices, on_device(): lax.all_gather(corner_piece, 'col', axis=1, tiled=True)[:, :panel_width]  42.4 us
    another operation x2, other arithmetic, factor_diag(): second_inv = jax.scipy.linalg.solve_triangular(second, identity, lower=True)  42 us
  transfers between devices with their start and end apart: 4, of which 4 were waited for; matrix products, arithmetic and copies ran while one was open for 1% of the time, Pallas kernels for 0%

commit v1 on v0

v1 whole, which is shorter than its diff:
```python
import jax
import jax.numpy as jnp
from jax import lax
from jax.experimental import pallas as pl
from jax.experimental.pallas import tpu as pltpu
from jax.sharding import PartitionSpec as P

BLK = 128
PB = 4
NB = 2 * PB
PW = NB * BLK
SUB = 16

precise = lax.Precision.HIGHEST
fast = lax.Precision.HIGH


def dot_nn(a, b):
    return jnp.dot(a, b, precision=precise, preferred_element_type=jnp.float32)


def dot_nt(a, b):
    return lax.dot_general(
        a, b, (((1,), (1,)), ((), ())), precision=precise, preferred_element_type=jnp.float32
    )


def lane_copy(x, lane):
    return jnp.broadcast_to(x[:, lane : lane + 1], (8, BLK))


def row_copy(x, row):
    return jnp.broadcast_to(x[row : row + 1, :], (8, BLK))


def reciprocal(x):
    guess = pl.reciprocal(x, approx=True)
    return guess * (2.0 - x * guess)


def invert_base(tiles):
    sub = lax.broadcasted_iota(jnp.int32, (8, BLK), 0)
    lane = lax.broadcasted_iota(jnp.int32, (8, BLK), 1)
    tiles = list(tiles)
    groups = SUB // 8
    result = [None] * 16
    for panel in range(BLK // SUB):
        c0 = panel * SUB
        g0 = panel * groups
        inside = (lane >= c0) & (lane < c0 + SUB)
        cols = [[lane_copy(tiles[g0 + g], c0 + k) for g in range(groups)] for k in range(SUB)]
        rows = [
            jnp.where(inside, jnp.where(lane == sub + (c0 + 8 * g), 1.0, 0.0), tiles[g0 + g])
            for g in range(groups)
        ]
        upper = list(rows)
        pivots = [jnp.ones((8, BLK), jnp.float32)] * groups
        below = {
            (g, k): lane_copy(tiles[g], c0 + k) for g in range(g0 + groups, 16) for k in range(SUB)
        }
        for p in range(SUB):
            gp, sp = p // 8, p % 8
            here = sub == sp
            pivot = row_copy(cols[p][gp], sp)
            inv = reciprocal(pivot)
            pivots[gp] = jnp.where(here, pivot, pivots[gp])
            upper[gp] = jnp.where(here, rows[gp], upper[gp])
            for k in range(p + 1, SUB):
                scaled = row_copy(cols[k][gp], sp) * inv
                for g in range(groups):
                    new = cols[k][g] - cols[p][g] * scaled
                    cols[k][g] = jnp.where(here, scaled, new) if g == gp else new
            scaled = row_copy(rows[gp], sp) * inv
            for g in range(groups):
                new = rows[g] - cols[p][g] * scaled
                rows[g] = jnp.where(here, scaled, new) if g == gp else new
        for g in range(groups):
            result[g0 + g] = jnp.where(
                lane <= sub + (c0 + 8 * g), upper[g] * lax.rsqrt(pivots[g]), 0.0
            )
        if g0 + groups < 16:
            solved = [row_copy(rows[k // 8], k % 8) for k in range(SUB)]
            for g in range(g0 + groups, 16):
                tile = jnp.where(inside, 0.0, tiles[g])
                for k in range(SUB):
                    tile = tile - below[g, k] * solved[k]
                tiles[g] = tile
    return result


def factor_kernel(d_ref, f_ref, v_ref, work, base, sweep):
    work[...] = d_ref[...]
    f_ref[...] = jnp.zeros_like(f_ref)
    lane = lax.broadcasted_iota(jnp.int32, (BLK, PW), 1)
    lower = lax.broadcasted_iota(jnp.int32, (BLK, BLK), 1) <= lax.broadcasted_iota(
        jnp.int32, (BLK, BLK), 0
    )

    def step(k, carry):
        here = pl.ds(pl.multiple_of(k * BLK, BLK), BLK)
        tiles = invert_base([work[k, 8 * g : 8 * g + 8, here] for g in range(16)])
        for g in range(16):
            base[8 * g : 8 * g + 8, :] = tiles[g]
        inv = base[...]
        f_ref[k, :, here] = jnp.where(lower, dot_nt(work[k, :, here], inv), 0.0)
        sweep[...] = dot_nn(inv, work[k])
        sweep[:, here] = inv
        v_ref[k] = jnp.where(lane < (k + 1) * BLK, sweep[...], 0.0)

        def row(i, inner):
            below = dot_nt(work[i, :, here], inv)
            f_ref[i, :, here] = below
            work[i, :, here] = jnp.zeros((BLK, BLK), jnp.float32)
            work[i] = work[i] - dot_nn(below, sweep[...])
            return inner

        lax.fori_loop(k + 1, NB, row, 0)
        return carry

    lax.fori_loop(0, NB, step, 0)


def factor_diag(diagonal):
    shape = (NB, BLK, PW)
    factor, inverse = pl.pallas_call(
        factor_kernel,
        out_shape=[jax.ShapeDtypeStruct(shape, jnp.float32)] * 2,
        scratch_shapes=[
            pltpu.VMEM(shape, jnp.float32),
            pltpu.VMEM((BLK, BLK), jnp.float32),
            pltpu.VMEM((BLK, PW), jnp.float32),
        ],
        compiler_params=pltpu.CompilerParams(vmem_limit_bytes=48 * 2**20),
        cost_estimate=pl.CostEstimate(
            flops=70 * 10**9, bytes_accessed=200 * 10**6, transcendentals=0
        ),
    )(diagonal)
    return factor, inverse.reshape(PW, PW)


def on_device(matrix, pattern):
    rows = lax.axis_size("row")
    cols = lax.axis_size("col")
    row = lax.axis_index("row")
    col = lax.axis_index("col")
    half = PB * BLK
    local_rows = matrix.shape[0]
    row_blocks = local_rows // BLK
    col_blocks = matrix.shape[1] // BLK
    both = ("row", "col")

    def at(r, c):
        return r * cols + c

    same_core = [list(range(0, cols, 2)), list(range(1, cols, 2))]
    corner = lax.all_gather(matrix[:BLK, :BLK], "col", axis=0, axis_index_groups=same_core)
    corner = corner[: NB // 2]
    spread = lax.all_to_all(
        jnp.broadcast_to(corner[None], (rows,) + corner.shape), "row", 0, 0
    )[:NB]
    other = lax.ppermute(
        spread, both, [(at(r, c), at(r, c ^ 1)) for r in range(rows) for c in range(cols)]
    )
    odd = col % 2 == 1
    even_blocks = jnp.where(odd, other, spread)
    odd_blocks = jnp.where(odd, spread, other)
    diagonal = jnp.stack([even_blocks, odd_blocks], axis=2).reshape(NB, NB, BLK, BLK)
    diagonal = diagonal.transpose(0, 2, 1, 3).reshape(NB, BLK, PW)

    mid = local_rows // 2
    moved = lax.ppermute(
        matrix[mid:, :BLK], both, [(at(r, c), at(r, c + NB)) for r in range(rows) for c in range(NB)]
    )
    part = jnp.where(col < NB, matrix[:mid, :BLK], moved)
    panel_cols = lax.all_gather(part, "col", axis=0)

    pattern_grid = pattern.reshape(2, row_blocks, rows)
    own = lax.dynamic_index_in_dim(pattern_grid, row, axis=2, keepdims=False).astype(jnp.float32)
    masks = jnp.repeat(own, BLK, axis=1)

    def natural(x):
        return x.transpose(1, 0, 2).reshape(x.shape[1], PW)

    masked = jnp.concatenate([natural(panel_cols[:NB]), natural(panel_cols[NB:])], axis=0)
    masked = jnp.concatenate(
        [masked[:, :half] * masks[0][:, None], masked[:, half:] * masks[1][:, None]], axis=1
    )

    span = col_blocks * BLK
    share = span // rows
    own_share = lax.dynamic_slice_in_dim(masked, col * share, share, axis=0)
    got_share = lax.ppermute(
        own_share, both, [(at(r, c), at(c, r)) for r in range(rows) for c in range(cols)]
    )
    partner_masked = lax.all_gather(got_share, "row", axis=0, tiled=True)

    factor, inverse = factor_diag(diagonal)
    solved = jnp.einsum("rk,wk->rw", masked, inverse, precision=fast)
    factor_rows = lax.dynamic_index_in_dim(factor, jnp.minimum(row, NB - 1), axis=0, keepdims=False)
    top = jnp.where(row < NB, factor_rows, solved[:BLK])
    panel = jnp.concatenate([top, solved[BLK:]], axis=0)
    partner = jnp.einsum("rk,wk->rw", partner_masked, inverse, precision=fast)
    update = jnp.einsum("rw,cw->rc", panel, partner, precision=fast)
    row_ids = jnp.arange(row_blocks, dtype=jnp.int32) * rows + row
    col_ids = jnp.arange(col_blocks, dtype=jnp.int32) * cols + col
    keep = jnp.repeat(row_ids >= NB, BLK)[:, None] & jnp.repeat(col_ids >= NB, BLK)[None, :]
    schur = jnp.where(keep, matrix - update, jnp.zeros_like(update))
    return (panel, schur)


def solution(mesh):
    in_specs = (P("row", "col"), P())
    out_specs = (P("row", None), P("row", "col"))
    return jax.shard_map(
        on_device, mesh=mesh, in_specs=in_specs, out_specs=out_specs, check_vma=False
    )
```

time: 663 us -> 300 us (0.45)
  the two profiles are of different devices: /device:TPU:1 before, /device:TPU:6 now
where the time goes in v1:
time: 300 us; the launch traced here: 299 us
  blocking collectives  85.5 us (28%)
  Pallas kernels  67.6 us (23%)
  waiting for transfers between devices  50.6 us (17%)
  matrix products  27 us (9%)
  local copies, waits for them, and re-layouts  21.8 us (7%)
  other arithmetic  18.1 us (6%)
  starting transfers between devices  14.3 us (5%)
  between operations  14.2 us (5%)
    pallas_call x1, Pallas kernels, factor_diag(): pl.pallas_call(factor_kernel, out_shape=[jax.ShapeDtypeStruct(shape, jnp....  67.6 us
    all_to_all x1, blocking collectives, on_device(): lax.all_to_all(jnp.broadcast_to(corner[None], (rows,) + corner.shape), 'r...  51.3 us
    ppermute x1, waiting for transfers between devices, on_device(): lax.ppermute(own_share, both, [(at(r, c), at(c, r)) for r in range(rows)...  41.7 us
    all_gather x1, blocking collectives, on_device(): lax.all_gather(matrix[:BLK, :BLK], 'col', axis=0, axis_index_groups=same_...  34.1 us
    dot_general x1, matrix products, on_device(): solved = jnp.einsum('rk,wk->rw', masked, inverse, precision=fast)  15.7 us
    ppermute x1, starting transfers between devices, on_device(): lax.ppermute(matrix[mid:, :BLK], both, [(at(r, c), at(r, c + NB)) for r i...  9.11 us
    dot_general x1, matrix products, on_device(): partner = jnp.einsum('rk,wk->rw', partner_masked, inverse, precision=fast)  6.46 us
  transfers between devices with their start and end apart: 5, of which 3 were waited for; matrix products, arithmetic and copies ran while one was open for 12% of the time, Pallas kernels for 23%

profile of v1, /device:TPU:6, one launch (start us, length us, event | category | flops | bytes accessed | tf_op | source)
XLA Modules:
  0.0 299.1 jit_solution(4692525536209487832)
XLA Ops:
  7.2 1.0 slice.53
  8.2 9.1 %collective-permute-start.1 = (f32[512,128]{1,0:T(8,128)S(1)}, f32[512,128]{1,0:T(8,128)S(1)}, u32[]{:S(2)}, u32[]{:S(2)}) collective-permute-start(f32[512,128]{1,0:T(8,128)S(1)} %slice.53), channel_id=1, source_target_pairs={{0,8},{1,9},{2,10},{3,11},{4,12},{5,13},{6,14},{7,15},{16,24},{17,... | collective-permute-start | bytes 786440 | tf_op jit(solution)/shard_map/ppermute | solution.py:171
  17.3 5.5 %collective-permute-done.1 = f32[512,128]{1,0:T(8,128)S(1)} collective-permute-done((f32[512,128]{1,0:T(8,128)S(1)}, f32[512,128]{1,0:T(8,128)S(1)}, u32[]{:S(2)}, u32[]{:S(2)}) %collective-permute-start.1) | collective-permute-done | bytes 262176 | tf_op jit(solution)/shard_map/ppermute | solution.py:171
  22.8 1.7 slice_select_fusion.1
  24.6 0.8 slice.49
  25.4 34.1 %all-gather = f32[1024,128]{1,0:T(8,128)S(1)} all-gather(f32[128,128]{1,0:T(8,128)S(1)} %slice.49), channel_id=2, replica_groups={{0,2,4,6,8,10,12,14},{1,3,5,7,9,11,13,15},{16,18,20,22,24,26,28,30},{17..., dimensions={0}, use_global_device_ids=true | all-gather | bytes 589824 | tf_op jit(solution)/shard_map/all_gather | solution.py:156
  59.6 0.2 copy.15
  59.8 0.8 broadcast_in_dim.24
  60.6 51.3 %all_to_all.5 = f32[16,4,128,128]{3,1,2,0:T(4,128)S(1)} all-to-all(f32[16,4,128,128]{3,1,2,0:T(4,128)S(1)} %broadcast_in_dim.24), channel_id=1, replica_groups=mesh['row'=16,'col'=16] {'row'}, dimensions={0} | all-to-all | bytes 8388608 | tf_op jit(solution)/shard_map/all_to_all | solution.py:158
  111.9 2.0 copy-done.1
  113.9 0.1 slice.68
  114.1 0.1 collective-permute-start
  114.2 0.4 copy-done.7
  115.1 3.4 %collective-permute-done = f32[8,4,128,128]{3,1,2,0:T(4,128)} collective-permute-done((f32[8,4,128,128]{3,1,2,0:T(4,128)S(1)}, f32[8,4,128,128]{3,1,2,0:T(4,128)}, u32[]{:S(2)}, u32[]{:S(2)}) %collective-permute-start) | collective-permute-done | bytes 2097184 | tf_op jit(solution)/shard_map/ppermute | solution.py:161
  118.5 5.1 %broadcast_select_fusion.1 = (f32[8,4,128,128]{3,1,2,0:T(4,128)}, f32[8,4,128,128]{3,1,2,0:T(4,128)}) fusion(f32[8,4,128,128]{3,1,2,0:T(4,128)} %collective-permute-done, pred[]{:T(512)S(6)} %eq.5, f32[16,4,128,128]{3,1,2,0:T(4,128)} %copy-done.1), kind=kLoop, calls=%fused_computation.14 | loop fusion | flops 1048576 | bytes 8388609 | tf_op jit(solution)/shard_map/jit(_where)/select_n | solution.py:165
  123.6 3.8 %fusion.6 = (f32[4096,128]{1,0:T(8,128)S(1)}, f32[4096,128]{1,0:T(8,128)}) fusion(f32[8192,128]{1,0:T(8,128)} %all-gather.7.cloned.1.call-done), kind=kLoop, calls=%fused_computation.28 | loop fusion | bytes 8388608 | tf_op jit(solution)/shard_map/slice | solution.py:184
  127.4 2.9 copy.18
  130.3 1.8 copy.17
  132.1 2.6 fusion.2
  134.8 0.2 fusion.4
  135.0 1.1 copy-done.2
  136.1 5.1 %collective-permute-start.2 = (f32[32,1024]{0,1:T(8,128)S(1)}, f32[32,1024]{0,1:T(8,128)S(1)}, u32[]{:S(2)}, u32[]{:S(2)}) collective-permute-start(f32[32,1024]{0,1:T(8,128)S(1)} %fusion.4), channel_id=1, source_target_pairs={{0,0},{1,16},{2,32},{3,48},{4,64},{5,80},{6,96},{7,112},{8,128},{9... | collective-permute-start | bytes 393224 | tf_op jit(solution)/shard_map/ppermute | solution.py:192
  141.2 5.7 %pad_maximum_fusion.2 = f32[8,4,2,128,128]{4,2,1,3,0:T(2,128)} fusion(f32[8,4,1,128,128]{4,2,1,3,0:T(1,128)S(1)} %bitcast.44, f32[8,4,1,128,128]{4,2,1,3,0:T(1,128)S(1)} %bitcast.43), kind=kLoop, calls=%fused_computation.4 | loop fusion | flops 1048576 | bytes 8388608 | tf_op jit(solution)/shard_map/stack | solution.py:167
  147.0 4.9 %reshape.42.d_ref = f32[8,128,1024]{2,1,0:T(8,128)} reshape(f32[8,128,8,128]{3,2,1,0:T(8,128)} %bitcast.38) | data formatting | bytes 8388608 | tf_op jit(solution)/shard_map/reshape | solution.py:168
  151.9 41.7 %collective-permute-done.2 = f32[32,1024]{0,1:T(8,128)S(1)} collective-permute-done((f32[32,1024]{0,1:T(8,128)S(1)}, f32[32,1024]{0,1:T(8,128)S(1)}, u32[]{:S(2)}, u32[]{:S(2)}) %collective-permute-start.2) | collective-permute-done | bytes 131104 | tf_op jit(solution)/shard_map/ppermute | solution.py:192
  193.6 0.8 copy.20
  194.5 67.6 %shard_map.41 = (f32[8,128,1024]{2,1,0:T(8,128)S(1)}, f32[8,128,1024]{2,1,0:T(8,128)}) custom-call(f32[8,128,1024]{2,1,0:T(8,128)} %reshape.42.d_ref), custom_call_target="tpu_custom_call" | custom-call | flops 70000001024 | bytes 200000000 | tf_op jit(solution)/shard_map/pallas_call | solution.py:125
  262.0 15.7 %fusion = f32[1024,1024]{1,0:T(8,128)S(1)} fusion(f32[1024,1024]{1,0:T(8,128)} %bitcast.45, f32[1024,512]{0,1:T(8,128)S(1)} %copy-done.3, f32[1024,512]{0,1:T(8,128)S(1)} %get-tuple-element.8), kind=kOutput, calls=%fused_computation.3 | convolution fusion | flops 6443499520 | bytes 12582912 | tf_op jit(solution)/shard_map/rk,wk->rw/dot_general | solution.py:198
  277.7 0.5 slice.76
  278.3 2.6 pad_maximum_fusion.3
  280.9 6.5 %fusion.7 = f32[512,1024]{1,0:T(8,128)S(1)} fusion(f32[512,1024]{1,0:T(8,128)} %all-gather.5.cloned.1.call-done, f32[1024,1024]{1,0:T(8,128)} %bitcast.46), kind=kOutput, calls=%fused_computation.29 | convolution fusion | flops 3221225472 | bytes 8388608 | tf_op jit(solution)/shard_map/rk,wk->rw/dot_general | solution.py:202
  287.4 4.9 %subtract_select_fusion = f32[1024,512]{1,0:T(8,128)} fusion(f32[1024,512]{1,0:T(8,128)S(1)} %copy-done.6, f32[1024,1024]{1,0:T(8,128)S(1)} %copy-done, f32[512,1024]{1,0:T(8,128)S(1)} %fusion.7, pred[512]{0:T(512)(128)(4,1)S(1)} %broadcast_bitcast_fusion.3, pred[1024]{0:T(1024)(128)(4,1)S(1)} %broadcast_bitcast_fusion.2), kind=kOutput, calls=%fused_computation.12 | convolution fusion | flops 3222798336 | bytes 10487296 | tf_op jit(solution)/shard_map/rw,cw->rc/dot_general | solution.py:203
  (31 shorter events, 0.7 us)
Async XLA Ops:
  7.2 116.4 %all-gather.7.cloned.1.call-start = ((), (), s32[]{:S(2)}) async-start(), calls=%async_computation.2 | async-start | bytes 4456448 | tf_op jit(solution)/shard_map/all_gather | solution.py:175
  8.2 14.6 %collective-permute-start.1 = (f32[512,128]{1,0:T(8,128)S(1)}, f32[512,128]{1,0:T(8,128)S(1)}, u32[]{:S(2)}, u32[]{:S(2)}) collective-permute-start(f32[512,128]{1,0:T(8,128)S(1)} %slice.53), channel_id=1, source_target_pairs={{0,8},{1,9},{2,10},{3,11},{4,12},{5,13},{6,14},{7,15},{16,24},{17,... | collective-permute-start | bytes 786440 | tf_op jit(solution)/shard_map/ppermute | solution.py:171
  24.5 256.4 %all-gather.5.cloned.1.call-start = ((), (), s32[]{:S(2)}) async-start(), calls=%async_computation.1 | async-start | bytes 2228224 | tf_op jit(solution)/shard_map/all_gather | solution.py:195
  111.9 2.0 copy-start.1
  113.9 0.7 copy-start.7
  114.1 4.4 %collective-permute-start = (f32[8,4,128,128]{3,1,2,0:T(4,128)S(1)}, f32[8,4,128,128]{3,1,2,0:T(4,128)}, u32[]{:S(2)}, u32[]{:S(2)}) collective-permute-start(f32[8,4,128,128]{3,1,2,0:T(4,128)S(1)} %slice.68), channel_id=1, source_target_pairs={{0,1},{1,0},{2,3},{3,2},{4,5},{5,4},{6,7},{7,6},{8,9},{9,8},{10,11... | collective-permute-start | bytes 6291464 | tf_op jit(solution)/shard_map/ppermute | solution.py:161
  134.7 1.4 copy-start.2
  134.8 6.5 %copy-start.4 = (f32[8,4,128,128]{3,1,2,0:T(4,128)S(1)}, f32[8,4,128,128]{3,1,2,0:T(4,128)}, u32[]{:S(2)}) copy-start(f32[8,4,128,128]{3,1,2,0:T(4,128)} %get-tuple-element.6) | copy-start | bytes 6291460
  134.8 6.5 %copy-start.5 = (f32[8,4,128,128]{3,1,2,0:T(4,128)S(1)}, f32[8,4,128,128]{3,1,2,0:T(4,128)}, u32[]{:S(2)}) copy-start(f32[8,4,128,128]{3,1,2,0:T(4,128)} %get-tuple-element.7) | copy-start | bytes 6291460
  136.1 57.5 %collective-permute-start.2 = (f32[32,1024]{0,1:T(8,128)S(1)}, f32[32,1024]{0,1:T(8,128)S(1)}, u32[]{:S(2)}, u32[]{:S(2)}) collective-permute-start(f32[32,1024]{0,1:T(8,128)S(1)} %fusion.4), channel_id=1, source_target_pairs={{0,0},{1,16},{2,32},{3,48},{4,64},{5,80},{6,96},{7,112},{8,128},{9... | collective-permute-start | bytes 393224 | tf_op jit(solution)/shard_map/ppermute | solution.py:192
  194.5 67.6 %copy-start.3 = (f32[1024,512]{0,1:T(8,128)S(1)}, f32[1024,512]{0,1:T(8,128)}, u32[]{:S(2)}) copy-start(f32[1024,512]{0,1:T(8,128)} %copy-done.2) | copy-start | bytes 6291460
  280.9 6.5 %copy-start.6 = (f32[1024,512]{1,0:T(8,128)S(1)}, f32[1024,512]{1,0:T(8,128)}, u32[]{:S(2)}) copy-start(f32[1024,512]{1,0:T(8,128)} %param.2) | copy-start | bytes 6291460
  280.9 6.5 %copy-start = (f32[1024,1024]{1,0:T(8,128)S(1)}, f32[1024,1024]{1,0:T(8,128)}, u32[]{:S(2)}) copy-start(f32[1024,1024]{1,0:T(8,128)} %pad_maximum_fusion.3) | copy-start | bytes 12582916
Sparse Core Ops, SparseCore 0:
  24.7 50.4 all-gather.6
  194.6 43.5 all-gather.4

commit v2 on v1

--- a/solution.py
+++ b/solution.py
@@ -1,5 +1,6 @@
 import jax
 import jax.numpy as jnp
+import numpy as np
 from jax import lax
 from jax.experimental import pallas as pl
 from jax.experimental.pallas import tpu as pltpu
@@ -10,9 +11,19 @@
 NB = 2 * PB
 PW = NB * BLK
 SUB = 16
+SLOTS = 3
+HOLD = [
+    [[0, 2, 4], [1]],
+    [[2, 6], [1, 3, 7]],
+    [[2, 4, 6], [3, 5]],
+    [[0, 4, 6], [3, 5]],
+    [[4, 6], [1, 7]],
+    [[0, 4], [1, 5]],
+    [[0, 6], [5, 7]],
+    [[0, 2], [3, 5, 7]],
+]
 
 precise = lax.Precision.HIGHEST
-fast = lax.Precision.HIGH
 
 
 def dot_nn(a, b):
@@ -88,8 +99,21 @@
     return result
 
 
-def factor_kernel(d_ref, f_ref, v_ref, work, base, sweep):
-    work[...] = d_ref[...]
+def split(x):
+    high = x.astype(jnp.bfloat16)
+    return high, (x - high.astype(jnp.float32)).astype(jnp.bfloat16)
+
+
+def factor_kernel(odd_ref, own_ref, other_ref, f_ref, high_ref, low_ref, work, base, sweep):
+    odd = odd_ref[0] == 1
+    for i in range(NB):
+        for parity in range(2):
+            for slot, j in enumerate(HOLD[i][parity]):
+                mine, theirs = own_ref[i, slot], other_ref[i, slot]
+                block = jnp.where(odd, mine, theirs) if parity else jnp.where(odd, theirs, mine)
+                work[i, :, j * BLK : (j + 1) * BLK] = block
+                if i != j:
+                    work[j, :, i * BLK : (i + 1) * BLK] = block.T
     f_ref[...] = jnp.zeros_like(f_ref)
     lane = lax.broadcasted_iota(jnp.int32, (BLK, PW), 1)
     lower = lax.broadcasted_iota(jnp.int32, (BLK, BLK), 1) <= lax.broadcasted_iota(
@@ -105,7 +129,9 @@
         f_ref[k, :, here] = jnp.where(lower, dot_nt(work[k, :, here], inv), 0.0)
         sweep[...] = dot_nn(inv, work[k])
         sweep[:, here] = inv
-        v_ref[k] = jnp.where(lane < (k + 1) * BLK, sweep[...], 0.0)
+        high, low = split(jnp.where(lane < (k + 1) * BLK, sweep[...], 0.0))
+        high_ref[k] = high
+        low_ref[k] = low
 
         def row(i, inner):
             below = dot_nt(work[i, :, here], inv)
@@ -120,11 +146,18 @@
     lax.fori_loop(0, NB, step, 0)
 
 
-def factor_diag(diagonal):
+def factor_diag(odd, own, other):
     shape = (NB, BLK, PW)
-    factor, inverse = pl.pallas_call(
+    vmem = pl.BlockSpec(memory_space=pltpu.VMEM)
+    return pl.pallas_call(
         factor_kernel,
-        out_shape=[jax.ShapeDtypeStruct(shape, jnp.float32)] * 2,
+        out_shape=[
+            jax.ShapeDtypeStruct(shape, jnp.float32),
+            jax.ShapeDtypeStruct(shape, jnp.bfloat16),
+            jax.ShapeDtypeStruct(shape, jnp.bfloat16),
+        ],
+        in_specs=[pl.BlockSpec(memory_space=pltpu.SMEM), vmem, vmem],
+        out_specs=[vmem, vmem, vmem],
         scratch_shapes=[
             pltpu.VMEM(shape, jnp.float32),
             pltpu.VMEM((BLK, BLK), jnp.float32),
@@ -134,8 +167,141 @@
         cost_estimate=pl.CostEstimate(
             flops=70 * 10**9, bytes_accessed=200 * 10**6, transcendentals=0
         ),
-    )(diagonal)
-    return factor, inverse.reshape(PW, PW)
+    )(odd, own, other)
+
+
+def dot3(a, b):
+    def term(x, y):
+        return lax.dot_general(x, y, (((1,), (1,)), ((), ())), preferred_element_type=jnp.float32)
+
+    return term(a[0], b[0]) + (term(a[0], b[1]) + term(a[1], b[0]))
+
+
+TILE = 256
+STEP = 256
+
+
+def tail_kernel(
+    at_ref,
+    pattern_ref,
+    w_ref,
+    wq_ref,
+    m_ref,
+    f_ref,
+    vh_ref,
+    vl_ref,
+    p_ref,
+    s_ref,
+    ah,
+    al,
+    ph,
+    pw,
+    qh,
+    ql,
+):
+    tile = pl.program_id(0)
+    row, col = at_ref[0], at_ref[1]
+    per = TILE // BLK
+
+    def masked(j, first_block, owner, get):
+        for b in range(per):
+            entry = pattern_ref[j // PB, (first_block + b) * 16 + owner].astype(jnp.float32)
+            high, low = split(get(j, b) * entry)
+            ah[b * BLK : (b + 1) * BLK, j * BLK : (j + 1) * BLK] = high
+            al[b * BLK : (b + 1) * BLK, j * BLK : (j + 1) * BLK] = low
+
+    def solve(store):
+        for n in range(PW // STEP):
+            rows = slice(n * STEP, (n + 1) * STEP)
+            depth = slice(0, (n + 1) * STEP)
+            store(
+                rows,
+                dot3((ah[:, depth], al[:, depth]), (vh_ref[rows, depth], vl_ref[rows, depth])),
+            )
+
+    @pl.when(tile == 0)
+    def _():
+        for h in range(2):
+            for j in range(NB):
+                masked(
+                    j, per * h, col, lambda j, b: wq_ref[2 * j + h, b * BLK : (b + 1) * BLK, :]
+                )
+
+            def keep(cols, value):
+                high, low = split(value)
+                qh[h * TILE : (h + 1) * TILE, cols] = high
+                ql[h * TILE : (h + 1) * TILE, cols] = low
+
+            solve(keep)
+
+    for j in range(NB):
+        masked(j, per * tile, row, lambda j, b: w_ref[j, b * BLK : (b + 1) * BLK, :])
+
+    def put(cols, value):
+        p_ref[:, cols] = value
+
+    solve(put)
+
+    top = (tile == 0) & (row < NB)
+
+    @pl.when(top)
+    def _():
+        p_ref[:BLK, :] = f_ref[0]
+
+    high, low = split(p_ref[...])
+    ph[...] = high
+    pw[...] = low
+    update = dot3((ph[...], pw[...]), (qh[...], ql[...]))
+    s_ref[...] = m_ref[...] - update
+
+    @pl.when(col < NB)
+    def _():
+        s_ref[:, :BLK] = jnp.zeros((TILE, BLK), jnp.float32)
+
+    @pl.when(top)
+    def _():
+        s_ref[:BLK, :] = jnp.zeros((BLK, s_ref.shape[1]), jnp.float32)
+
+
+def tail(at, pattern, panel_cols, partner_cols, matrix, factor, high, low):
+    rows, width = matrix.shape
+    whole = lambda *_: (0, 0)
+    grid_spec = pltpu.PrefetchScalarGridSpec(
+        num_scalar_prefetch=2,
+        grid=(rows // TILE,),
+        in_specs=[
+            pl.BlockSpec((NB, TILE, BLK), lambda t, *_: (0, t, 0)),
+            pl.BlockSpec((2 * NB, TILE, BLK), lambda t, *_: (0, 0, 0)),
+            pl.BlockSpec((TILE, width), lambda t, *_: (t, 0)),
+            pl.BlockSpec((1, BLK, PW), lambda t, at, _: (jnp.minimum(at[0], NB - 1), 0, 0)),
+            pl.BlockSpec((PW, PW), whole),
+            pl.BlockSpec((PW, PW), whole),
+        ],
+        out_specs=[
+            pl.BlockSpec((TILE, PW), lambda t, *_: (t, 0)),
+            pl.BlockSpec((TILE, width), lambda t, *_: (t, 0)),
+        ],
+        scratch_shapes=[
+            pltpu.VMEM((TILE, PW), jnp.bfloat16),
+            pltpu.VMEM((TILE, PW), jnp.bfloat16),
+            pltpu.VMEM((TILE, PW), jnp.bfloat16),
+            pltpu.VMEM((TILE, PW), jnp.bfloat16),
+            pltpu.VMEM((width, PW), jnp.bfloat16),
+            pltpu.VMEM((width, PW), jnp.bfloat16),
+        ],
+    )
+    return pl.pallas_call(
+        tail_kernel,
+        grid_spec=grid_spec,
+        out_shape=[
+            jax.ShapeDtypeStruct((rows, PW), jnp.float32),
+            jax.ShapeDtypeStruct((rows, width), jnp.float32),
+        ],
+        compiler_params=pltpu.CompilerParams(vmem_limit_bytes=48 * 2**20),
+        cost_estimate=pl.CostEstimate(
+            flops=10 * 10**9, bytes_accessed=20 * 10**6, transcendentals=0
+        ),
+    )(at, pattern, panel_cols, partner_cols, matrix, factor, high, low)
 
 
 def on_device(matrix, pattern):
@@ -143,68 +309,55 @@
     cols = lax.axis_size("col")
     row = lax.axis_index("row")
     col = lax.axis_index("col")
-    half = PB * BLK
-    local_rows = matrix.shape[0]
-    row_blocks = local_rows // BLK
-    col_blocks = matrix.shape[1] // BLK
     both = ("row", "col")
 
     def at(r, c):
         return r * cols + c
 
+    def pairs(target, width=cols):
+        return [(at(r, c), at(*target(r, c))) for r in range(rows) for c in range(width)]
+
+    first = matrix[:, :BLK]
+    panel_cols = lax.all_gather(first, "col", axis=0)
+
     same_core = [list(range(0, cols, 2)), list(range(1, cols, 2))]
-    corner = lax.all_gather(matrix[:BLK, :BLK], "col", axis=0, axis_index_groups=same_core)
-    corner = corner[: NB // 2]
-    spread = lax.all_to_all(
-        jnp.broadcast_to(corner[None], (rows,) + corner.shape), "row", 0, 0
-    )[:NB]
-    other = lax.ppermute(
-        spread, both, [(at(r, c), at(r, c ^ 1)) for r in range(rows) for c in range(cols)]
-    )
-    odd = col % 2 == 1
-    even_blocks = jnp.where(odd, other, spread)
-    odd_blocks = jnp.where(odd, spread, other)
-    diagonal = jnp.stack([even_blocks, odd_blocks], axis=2).reshape(NB, NB, BLK, BLK)
-    diagonal = diagonal.transpose(0, 2, 1, 3).reshape(NB, BLK, PW)
-
-    mid = local_rows // 2
-    moved = lax.ppermute(
-        matrix[mid:, :BLK], both, [(at(r, c), at(r, c + NB)) for r in range(rows) for c in range(NB)]
-    )
-    part = jnp.where(col < NB, matrix[:mid, :BLK], moved)
-    panel_cols = lax.all_gather(part, "col", axis=0)
-
-    pattern_grid = pattern.reshape(2, row_blocks, rows)
-    own = lax.dynamic_index_in_dim(pattern_grid, row, axis=2, keepdims=False).astype(jnp.float32)
-    masks = jnp.repeat(own, BLK, axis=1)
-
-    def natural(x):
-        return x.transpose(1, 0, 2).reshape(x.shape[1], PW)
-
-    masked = jnp.concatenate([natural(panel_cols[:NB]), natural(panel_cols[NB:])], axis=0)
-    masked = jnp.concatenate(
-        [masked[:, :half] * masks[0][:, None], masked[:, half:] * masks[1][:, None]], axis=1
-    )
-
-    span = col_blocks * BLK
-    share = span // rows
-    own_share = lax.dynamic_slice_in_dim(masked, col * share, share, axis=0)
-    got_share = lax.ppermute(
-        own_share, both, [(at(r, c), at(c, r)) for r in range(rows) for c in range(cols)]
-    )
-    partner_masked = lax.all_gather(got_share, "row", axis=0, tiled=True)
-
-    factor, inverse = factor_diag(diagonal)
-    solved = jnp.einsum("rk,wk->rw", masked, inverse, precision=fast)
-    factor_rows = lax.dynamic_index_in_dim(factor, jnp.minimum(row, NB - 1), axis=0, keepdims=False)
-    top = jnp.where(row < NB, factor_rows, solved[:BLK])
-    panel = jnp.concatenate([top, solved[BLK:]], axis=0)
-    partner = jnp.einsum("rk,wk->rw", partner_masked, inverse, precision=fast)
-    update = jnp.einsum("rw,cw->rc", panel, partner, precision=fast)
-    row_ids = jnp.arange(row_blocks, dtype=jnp.int32) * rows + row
-    col_ids = jnp.arange(col_blocks, dtype=jnp.int32) * cols + col
-    keep = jnp.repeat(row_ids >= NB, BLK)[:, None] & jnp.repeat(col_ids >= NB, BLK)[None, :]
-    schur = jnp.where(keep, matrix - update, jnp.zeros_like(update))
+    corner = jnp.broadcast_to(first[:BLK][None], (cols // 2, BLK, BLK))
+    corner = lax.all_to_all(corner, "col", 0, 0, axis_index_groups=same_core)
+    table = np.zeros((NB, 2, SLOTS), np.int32)
+    for i in range(NB):
+        for parity in range(2):
+            for slot, j in enumerate(HOLD[i][parity]):
+                table[i, parity, slot] = j // 2
+    chosen = jnp.asarray(table)[jnp.minimum(row, NB - 1), col % 2]
+    corner = jnp.stack(
+        [lax.dynamic_index_in_dim(corner, chosen[s], axis=0, keepdims=False) for s in range(SLOTS)]
+    )
+    own = lax.all_to_all(jnp.broadcast_to(corner[None], (rows,) + corner.shape), "row", 0, 0)
+    own = own[:NB]
+    other = lax.ppermute(own, both, pairs(lambda r, c: (r, c ^ 1)))
+
+    span = matrix.shape[1] // 2
+    shares = [
+        lax.ppermute(
+            first[h * span : (h + 1) * span], both, pairs(lambda r, c, h=h: (2 * c + h, r), NB)
+        )
+        for h in range(2)
+    ]
+    share = jnp.where(row % 2 == 0, shares[0], shares[1])
+    partner_cols = lax.all_gather(share, "row", axis=0)
+
+    factor, high, low = factor_diag((col % 2).astype(jnp.int32).reshape(1), own, other)
+    place = jnp.stack([row, col]).astype(jnp.int32)
+    panel, schur = tail(
+        place,
+        pattern,
+        panel_cols,
+        partner_cols,
+        matrix,
+        factor,
+        high.reshape(PW, PW),
+        low.reshape(PW, PW),
+    )
     return (panel, schur)
 
 

time: 300 us -> 225 us (0.75)
  the two profiles are of different devices: /device:TPU:6 before, /device:TPU:1 now
where the time goes in v2:
time: 225 us; the launch traced here: 224 us
  Pallas kernels  89.5 us (40%)
  blocking collectives  47.1 us (21%)
  starting transfers between devices  43.7 us (19%)
  between operations  19.9 us (9%)
  waiting for transfers between devices  14.7 us (7%)
  local copies, waits for them, and re-layouts  8.62 us (4%)
    pallas_call x1, Pallas kernels, factor_diag(): pl.pallas_call(factor_kernel, out_shape=[jax.ShapeDtypeStruct(shape, jnp....  67 us
    all_to_all x1, blocking collectives, on_device(): lax.all_to_all(jnp.broadcast_to(corner[None], (rows,) + corner.shape), 'r...  47.1 us
    all_to_all x1, starting transfers between devices, on_device(): corner = lax.all_to_all(corner, 'col', 0, 0, axis_index_groups=same_core)  28.5 us
    pallas_call x1, Pallas kernels, tail(): pl.pallas_call(tail_kernel, grid_spec=grid_spec, out_shape=[jax.ShapeDtyp...  22.5 us
    ppermute x2, starting transfers between devices, on_device(): lax.ppermute(first[h * span:(h + 1) * span], both, pairs(lambda r, c, h=h...  9.93 us
    all_to_all x1, waiting for transfers between devices, on_device(): corner = lax.all_to_all(corner, 'col', 0, 0, axis_index_groups=same_core)  9.39 us
    ppermute x1, starting transfers between devices, on_device(): other = lax.ppermute(own, both, pairs(lambda r, c: (r, c ^ 1)))  5.17 us
  transfers between devices with their start and end apart: 6, of which 3 were waited for; matrix products, arithmetic and copies ran while one was open for 2% of the time, Pallas kernels for 30%

profile of v2, /device:TPU:1, one launch (start us, length us, event | category | flops | bytes accessed | tf_op | source)
XLA Modules:
  0.0 224.3 jit_solution(1441800857954315837)
XLA Ops:
  7.2 0.0 copy-start
  7.2 0.0 all-gather.7.cloned.1.call-start
  7.2 1.1 fusion
  8.4 6.0 %collective-permute-start.1 = (f32[256,128]{1,0:T(8,128)S(1)}, f32[256,128]{1,0:T(8,128)S(1)}, u32[]{:S(2)}, u32[]{:S(2)}) collective-permute-start(f32[256,128]{1,0:T(8,128)S(1)} %get-tuple-element.8), channel_id=1, source_target_pairs={{0,16},{1,48},{2,80},{3,112},{4,144},{5,176},{6,208},{7,240},{16,1... | collective-permute-start | bytes 393224 | tf_op jit(solution)/shard_map/ppermute | solution.py:341
  14.4 3.9 %collective-permute-start = (f32[256,128]{1,0:T(8,128)S(1)}, f32[256,128]{1,0:T(8,128)S(1)}, u32[]{:S(2)}, u32[]{:S(2)}) collective-permute-start(f32[256,128]{1,0:T(8,128)S(1)} %get-tuple-element.9), channel_id=1, source_target_pairs={{0,0},{1,32},{2,64},{3,96},{4,128},{5,160},{6,192},{7,224},{16,1},... | collective-permute-start | bytes 393224 | tf_op jit(solution)/shard_map/ppermute | solution.py:341
  18.3 0.0 collective-permute-done.1
  18.3 2.4 %collective-permute-done = f32[256,128]{1,0:T(8,128)S(1)} collective-permute-done((f32[256,128]{1,0:T(8,128)S(1)}, f32[256,128]{1,0:T(8,128)S(1)}, u32[]{:S(2)}, u32[]{:S(2)}) %collective-permute-start) | collective-permute-done | bytes 131104 | tf_op jit(solution)/shard_map/ppermute | solution.py:341
  20.7 0.7 broadcast_select_fusion
  21.4 0.0 all-gather.7.cloned.1.call-update
  21.4 0.0 all-gather.5.cloned.1.call-start
  21.4 1.9 slice.30
  23.3 0.0 all-gather.5.cloned.1.call-update
  23.3 0.0 copy-done
  23.4 0.8 broadcast_in_dim.4
  24.2 28.5 %all-to-all-start = ((f32[8,128,128]{2,1,0:T(8,128)}), f32[8,128,128]{2,1,0:T(8,128)S(1)}, u32[]{:S(2)}, u32[]{:S(2)}) async-start(f32[8,128,128]{2,1,0:T(8,128)} %broadcast_in_dim.4), calls=%async_computation | async-start | bytes 1048576 | tf_op jit(solution)/shard_map/all_to_all | solution.py:325
  52.7 0.7 constant_dynamic-slice_fusion.3
  53.4 0.6 fusion.1
  59.8 9.4 %all-to-all-done = f32[8,128,128]{2,1,0:T(8,128)S(1)} async-done(((f32[8,128,128]{2,1,0:T(8,128)}), f32[8,128,128]{2,1,0:T(8,128)S(1)}, u32[]{:S(2)}, u32[]{:S(2)}) %all-to-all-start) | async-done | bytes 524320 | tf_op jit(solution)/shard_map/all_to_all | solution.py:325
  69.3 0.4 broadcast_in_dim.5
  69.6 47.1 %all_to_all.10 = f32[16,3,128,128]{3,2,1,0:T(8,128)S(1)} all-to-all(f32[16,3,128,128]{3,2,1,0:T(8,128)S(1)} %broadcast_in_dim.5), channel_id=1, replica_groups=mesh['row'=16,'col'=16] {'row'}, dimensions={0} | all-to-all | bytes 6291456 | tf_op jit(solution)/shard_map/all_to_all | solution.py:335
  116.7 0.1 slice.38.own_ref
  116.8 5.2 %collective-permute-start.2 = (f32[8,3,128,128]{3,2,1,0:T(8,128)S(1)}, f32[8,3,128,128]{3,2,1,0:T(8,128)S(1)}, u32[]{:S(2)}, u32[]{:S(2)}) collective-permute-start(f32[8,3,128,128]{3,2,1,0:T(8,128)S(1)} %slice.38.own_ref), channel_id=1, source_target_pairs={{0,1},{1,0},{2,3},{3,2},{4,5},{5,4},{6,7},{7,6},{8,9},{9,8},{10,11... | collective-permute-start | bytes 4718600 | tf_op jit(solution)/shard_map/ppermute | solution.py:337
  122.0 0.1 pad_add_fusion.at_ref
  122.1 3.0 %collective-permute-done.2.other_ref = f32[8,3,128,128]{3,2,1,0:T(8,128)S(1)} collective-permute-done((f32[8,3,128,128]{3,2,1,0:T(8,128)S(1)}, f32[8,3,128,128]{3,2,1,0:T(8,128)S(1)}, u32[]{:S(2)}, u32[]{:S(2)}) %collective-permute-start.2) | collective-permute-done | bytes 1572896 | tf_op jit(solution)/shard_map/ppermute | solution.py:337
  125.0 0.0 copy-start.2
  125.0 67.0 %shard_map.50 = (f32[8,128,1024]{2,1,0:T(8,128)}, bf16[8,128,1024]{2,1,0:T(8,128)(2,1)S(1)}, bf16[8,128,1024]{2,1,0:T(8,128)(2,1)}) custom-call(s32[1]{0:T(128)} %bitcast.4.odd_ref, f32[8,3,128,128]{3,2,1,0:T(8,128)S(1)} %slice.38.own_ref, f32[8,3,128,128]{3,2,1,0:T(8,128)S(1)} %collective-permute-done.2.other_ref), custom_call_target="tpu_custom_call" | custom-call | flops 70000001024 | bytes 200000000 | tf_op jit(solution)/shard_map/pallas_call | solution.py:152
  192.1 0.0 copy-start.3
  192.1 1.3 copy-done.3
  193.4 0.0 all-gather.7.cloned.1.call-done
  193.4 0.0 copy-done.2
  193.4 1.6 copy-done.1
  195.0 22.5 %shard_map.51 = (f32[1024,1024]{1,0:T(8,128)}, f32[1024,512]{1,0:T(8,128)}) custom-call(s32[2]{0:T(128)S(1)} %pad_add_fusion.at_ref, s32[2,128]{1,0:T(2,128)S(1)} %copy-done.2, f32[16,1024,128]{2,1,0:T(8,128)} %bitcast.12, f32[16,256,128]{2,1,0:T(8,128)S(1)} %bitcast.10, f32[1024,512]{1,0:T(8,128)S(1)} %copy-done, f32[8,128,1024]{2,1,0:T(8,128)} %get-tuple-element.5.f_ref, ...), custom_call_target="tpu_custom_call" | custom-call | flops 10000000000 | bytes 20000000 | tf_op jit(solution)/shard_map/pallas_call | solution.py:293
  (5 shorter events, 0.0 us)
Async XLA Ops:
  7.2 16.2 %copy-start = (f32[1024,512]{1,0:T(8,128)S(1)}, f32[1024,512]{1,0:T(8,128)}, u32[]{:S(2)}) copy-start(f32[1024,512]{1,0:T(8,128)} %m_ref.1) | copy-start | bytes 6291460
  7.2 186.2 %all-gather.7.cloned.1.call-start = ((), (), s32[]{:S(2)}) async-start(), calls=%async_computation.3 | async-start | bytes 2228224 | tf_op jit(solution)/shard_map/all_gather | solution.py:347
  8.4 10.0 %collective-permute-start.1 = (f32[256,128]{1,0:T(8,128)S(1)}, f32[256,128]{1,0:T(8,128)S(1)}, u32[]{:S(2)}, u32[]{:S(2)}) collective-permute-start(f32[256,128]{1,0:T(8,128)S(1)} %get-tuple-element.8), channel_id=1, source_target_pairs={{0,16},{1,48},{2,80},{3,112},{4,144},{5,176},{6,208},{7,240},{16,1... | collective-permute-start | bytes 393224 | tf_op jit(solution)/shard_map/ppermute | solution.py:341
  14.4 6.3 %collective-permute-start = (f32[256,128]{1,0:T(8,128)S(1)}, f32[256,128]{1,0:T(8,128)S(1)}, u32[]{:S(2)}, u32[]{:S(2)}) collective-permute-start(f32[256,128]{1,0:T(8,128)S(1)} %get-tuple-element.9), channel_id=1, source_target_pairs={{0,0},{1,32},{2,64},{3,96},{4,128},{5,160},{6,192},{7,224},{16,1},... | collective-permute-start | bytes 393224 | tf_op jit(solution)/shard_map/ppermute | solution.py:341
  21.4 172.0 %all-gather.5.cloned.1.call-start = ((), (), s32[]{:S(2)}) async-start(), calls=%async_computation.2 | async-start | bytes 8912896 | tf_op jit(solution)/shard_map/all_gather | solution.py:321
  24.2 45.0 %all-to-all-start = ((f32[8,128,128]{2,1,0:T(8,128)}), f32[8,128,128]{2,1,0:T(8,128)S(1)}, u32[]{:S(2)}, u32[]{:S(2)}) async-start(f32[8,128,128]{2,1,0:T(8,128)} %broadcast_in_dim.4), calls=%async_computation | async-start | bytes 1048576 | tf_op jit(solution)/shard_map/all_to_all | solution.py:325
  116.8 8.2 %collective-permute-start.2 = (f32[8,3,128,128]{3,2,1,0:T(8,128)S(1)}, f32[8,3,128,128]{3,2,1,0:T(8,128)S(1)}, u32[]{:S(2)}, u32[]{:S(2)}) collective-permute-start(f32[8,3,128,128]{3,2,1,0:T(8,128)S(1)} %slice.38.own_ref), channel_id=1, source_target_pairs={{0,1},{1,0},{2,3},{3,2},{4,5},{5,4},{6,7},{7,6},{8,9},{9,8},{10,11... | collective-permute-start | bytes 4718600 | tf_op jit(solution)/shard_map/ppermute | solution.py:337
  125.0 68.4 %copy-start.2 = (s32[2,128]{1,0:T(2,128)S(1)}, s32[2,128]{1,0:T(2,128)}, u32[]{:S(2)}) copy-start(s32[2,128]{1,0:T(2,128)} %pattern_ref.1) | copy-start | bytes 3076
  192.1 1.3 copy-start.3
  193.4 1.6 copy-start.1
Sparse Core Ops, SparseCore 0:
  21.5 93.0 all-gather.6
  117.0 54.1 all-gather.4

commit v3 on v2

v3 whole, which is shorter than its diff:
```python
import jax
import jax.numpy as jnp
from jax import lax
from jax.experimental import pallas as pl
from jax.experimental.pallas import tpu as pltpu
from jax.sharding import PartitionSpec as P

BLK = 128
PB = 4
NB = 2 * PB
PW = NB * BLK
SUB = 16
SLOTS = 3
HOLD = [
    [[0, 2, 4], [1]],
    [[2, 6], [1, 3, 7]],
    [[2, 4, 6], [3, 5]],
    [[0, 4, 6], [3, 5]],
    [[4, 6], [1, 7]],
    [[0, 4], [1, 5]],
    [[0, 6], [5, 7]],
    [[0, 2], [3, 5, 7]],
]


def split(x):
    high = x.astype(jnp.bfloat16)
    return high, (x - high.astype(jnp.float32)).astype(jnp.bfloat16)


def split3(x):
    high = x.astype(jnp.bfloat16)
    rest = x - high.astype(jnp.float32)
    mid = rest.astype(jnp.bfloat16)
    return high, mid, (rest - mid.astype(jnp.float32)).astype(jnp.bfloat16)


def left6(x):
    high, mid, low = split3(x)
    return jnp.concatenate([high, mid, high, mid, high, low], axis=1)


def right6(x, axis):
    high, mid, low = split3(x)
    return jnp.concatenate([high, high, mid, mid, low, high], axis=axis)


def dot_nn(a, b):
    return jnp.dot(a, b, preferred_element_type=jnp.float32)


def dot_nt(a, b):
    return lax.dot_general(a, b, (((1,), (1,)), ((), ())), preferred_element_type=jnp.float32)


def lane_copy(x, lane):
    return jnp.broadcast_to(x[:, lane : lane + 1], (8, BLK))


def row_copy(x, row):
    return jnp.broadcast_to(x[row : row + 1, :], (8, BLK))


def reciprocal(x):
    return pl.reciprocal(x, approx=True)


def invert_base(tiles):
    sub = lax.broadcasted_iota(jnp.int32, (8, BLK), 0)
    lane = lax.broadcasted_iota(jnp.int32, (8, BLK), 1)
    tiles = list(tiles)
    result = []
    for panel in range(BLK // 8):
        c0 = panel * 8
        inside = (lane >= c0) & (lane < c0 + 8)
        cols = [lane_copy(tiles[panel], c0 + k) for k in range(8)]
        rows = jnp.where(inside, jnp.where(lane == sub + c0, 1.0, 0.0), tiles[panel])
        upper = rows
        pivots = jnp.ones((8, BLK), jnp.float32)
        below = {(g, k): lane_copy(tiles[g], c0 + k) for g in range(panel + 1, 16) for k in range(8)}
        for p in range(0, 8, 2):
            one, two = sub == p, sub == p + 1
            pair = one | two
            a, b = row_copy(cols[p], p), row_copy(cols[p + 1], p)
            c = row_copy(cols[p + 1], p + 1)
            det = a * c - b * b
            inv_det, inv_a = reciprocal(det), reciprocal(a)
            aa, ab, bb = c * inv_det, b * inv_det, a * inv_det
            top, low = row_copy(rows, p), row_copy(rows, p + 1)
            pivots = jnp.where(one, a, jnp.where(two, det * inv_a, pivots))
            upper = jnp.where(one, top, jnp.where(two, low - b * inv_a * top, upper))

            def swept(x, y, target):
                u, v = aa * x - ab * y, bb * y - ab * x
                return jnp.where(pair, jnp.where(one, u, v), target - (cols[p] * u + cols[p + 1] * v))

            for k in range(p + 2, 8):
                cols[k] = swept(row_copy(cols[k], p), row_copy(cols[k], p + 1), cols[k])
            rows = swept(top, low, rows)
        result.append(jnp.where(lane <= sub + c0, upper * lax.rsqrt(pivots), 0.0))
        if panel < 15:
            solved = [row_copy(rows, k) for k in range(8)]
            for g in range(panel + 1, 16):
                parts = [below[g, k] * solved[k] for k in range(8)]
                while len(parts) > 1:
                    parts = [parts[m] + parts[m + 1] for m in range(0, len(parts), 2)]
                tiles[g] = jnp.where(inside, 0.0, tiles[g]) - parts[0]
    return result


def invert_into(base, block):
    for g, tile in enumerate(invert_base([block[8 * g : 8 * g + 8, :] for g in range(16)])):
        base[8 * g : 8 * g + 8, :] = tile


def lower_part(x):
    shape = (BLK, BLK)
    keep = lax.broadcasted_iota(jnp.int32, shape, 1) <= lax.broadcasted_iota(jnp.int32, shape, 0)
    return jnp.where(keep, x, 0.0)


def factor_steps(first, last, work, diag, head, base):
    def step(k, carry):
        here = pl.ds(pl.multiple_of(k * BLK, BLK), BLK)
        there = pl.ds(pl.multiple_of(k * BLK + BLK, BLK), BLK)
        inv, block = base[...], head[...]
        inv_left, inv_right = left6(inv), right6(inv, 1)
        below = dot_nt(left6(work[k + 1, :, here]), inv_right)
        beside = dot_nn(inv_left, right6(work[k, :, there], 0))
        following = work[k + 1, :, there] - dot_nn(left6(below), right6(beside, 0))
        head[...] = following
        tiles = invert_base([following[8 * g : 8 * g + 8, :] for g in range(16)])
        diag[k] = lower_part(dot_nt(left6(block), inv_right))
        work[k] = dot_nn(inv_left, right6(work[k], 0))
        work[k, :, here] = inv
        sweep = right6(work[k], 0)
        for i in range(1, NB):
            block = work[i, :, here]
            below = left6(jnp.where(i > k, dot_nt(left6(block), inv_right), 0.0))
            work[i, :, here] = jnp.where(i > k, 0.0, block)
            work[i] = work[i] - dot_nn(below, sweep)
        for g in range(16):
            base[8 * g : 8 * g + 8, :] = tiles[g]
        return carry

    lax.fori_loop(first, last, step, 0)


FIRST_STEPS = 3


def start_kernel(odd_ref, own_ref, other_ref, work, diag, head, base):
    odd = odd_ref[0] == 1
    for i in range(NB):
        for parity in range(2):
            for slot, j in enumerate(HOLD[i][parity]):
                parts = []
                for at in (i, i + NB):
                    mine, theirs = own_ref[at, slot], other_ref[at, slot]
                    parts.append(jnp.where(odd == (parity == 1), mine, theirs))
                block = jnp.concatenate(parts, axis=0)
                work[i, :, j * BLK : (j + 1) * BLK] = block
                if i != j:
                    work[j, :, i * BLK : (i + 1) * BLK] = block.T
    head[...] = work[0, :, :BLK]
    invert_into(base, head)
    factor_steps(0, FIRST_STEPS, work, diag, head, base)


def finish_kernel(w_in, d_in, h_in, b_in, work, diag, head, base):
    factor_steps(FIRST_STEPS, NB - 1, work, diag, head, base)
    last = NB - 1
    inv = base[...]
    diag[last] = lower_part(dot_nt(left6(head[...]), right6(inv, 1)))
    work[last] = dot_nn(left6(inv), right6(work[last], 0))
    work[last, :, last * BLK :] = inv


STATE = [
    jax.ShapeDtypeStruct((NB, BLK, PW), jnp.float32),
    jax.ShapeDtypeStruct((NB, BLK, BLK), jnp.float32),
    jax.ShapeDtypeStruct((BLK, BLK), jnp.float32),
    jax.ShapeDtypeStruct((BLK, BLK), jnp.float32),
]


def factor_call(kernel, scalars, operands, aliases, share):
    vmem = pl.BlockSpec(memory_space=pltpu.VMEM)
    return pl.pallas_call(
        kernel,
        out_shape=STATE,
        in_specs=[pl.BlockSpec(memory_space=pltpu.SMEM)] * len(scalars) + [vmem] * len(operands),
        out_specs=[vmem] * len(STATE),
        input_output_aliases=aliases,
        compiler_params=pltpu.CompilerParams(vmem_limit_bytes=32 * 2**20),
        cost_estimate=pl.CostEstimate(
            flops=share * 10**10, bytes_accessed=share * 25 * 10**6, transcendentals=0
        ),
    )(*scalars, *operands)


def dot3(a, b):
    def term(x, y):
        return lax.dot_general(x, y, (((1,), (1,)), ((), ())), preferred_element_type=jnp.float32)

    return term(a[0], b[0]) + (term(a[0], b[1]) + term(a[1], b[0]))


TILE = 256
STEP = 256


def tail_kernel(
    at_ref, pattern_ref, w_ref, wq_ref, m_ref, work, diag, p_ref, s_ref, ah, al, qh, ql, vh, vl
):
    tile = pl.program_id(0)
    row, col = at_ref[0], at_ref[1]
    per = TILE // BLK

    def masked(j, first_block, owner, get):
        for b in range(per):
            entry = pattern_ref[j // PB, (first_block + b) * 16 + owner].astype(jnp.float32)
            high, low = split(get(j, b) * entry)
            ah[b * BLK : (b + 1) * BLK, j * BLK : (j + 1) * BLK] = high
            al[b * BLK : (b + 1) * BLK, j * BLK : (j + 1) * BLK] = low

    def solve(store):
        for n in range(PW // STEP):
            rows = slice(n * STEP, (n + 1) * STEP)
            depth = slice(0, (n + 1) * STEP)
            store(rows, dot3((ah[:, depth], al[:, depth]), (vh[rows, depth], vl[rows, depth])))

    @pl.when(tile == 0)
    def _():
        lane = lax.broadcasted_iota(jnp.int32, (BLK, PW), 1)
        for k in range(NB):
            high, low = split(jnp.where(lane < (k + 1) * BLK, work[k], 0.0))
            vh[k * BLK : (k + 1) * BLK, :] = high
            vl[k * BLK : (k + 1) * BLK, :] = low
        for h in range(qh.shape[0] // TILE):
            for j in range(NB):
                masked(
                    j,
                    per * h,
                    col,
                    lambda j, b: wq_ref[(2 * j + h) ^ col, b * BLK : (b + 1) * BLK, :],
                )

            def keep(cols, value):
                high, low = split(value)
                qh[h * TILE : (h + 1) * TILE, cols] = high
                ql[h * TILE : (h + 1) * TILE, cols] = low

            solve(keep)

    for j in range(NB):
        masked(j, per * tile, row, lambda j, b: w_ref[j, b * BLK : (b + 1) * BLK, :])

    def put(cols, value):
        p_ref[:, cols] = value

    solve(put)

    top = (tile == 0) & (row < NB)

    @pl.when(top)
    def _():
        here = pl.ds(pl.multiple_of(row * BLK, BLK), BLK)
        for k in range(NB):
            block = jnp.where(k < row, work[k, :, here].T, 0.0)
            p_ref[:BLK, k * BLK : (k + 1) * BLK] = jnp.where(k == row, diag[row], block)

    s_ref[...] = m_ref[...] - dot3(split(p_ref[...]), (qh[...], ql[...]))

    @pl.when(col < NB)
    def _():
        s_ref[:, :BLK] = jnp.zeros((TILE, BLK), jnp.float32)

    @pl.when(top)
    def _():
        s_ref[:BLK, :] = jnp.zeros((BLK, s_ref.shape[1]), jnp.float32)


def tail(at, pattern, panel_cols, partner_cols, matrix, work, diag):
    rows, width = matrix.shape
    pieces = partner_cols.shape
    grid_spec = pltpu.PrefetchScalarGridSpec(
        num_scalar_prefetch=2,
        grid=(rows // TILE,),
        in_specs=[
            pl.BlockSpec((NB, TILE, BLK), lambda t, *_: (0, t, 0)),
            pl.BlockSpec(pieces, lambda t, *_: (0, 0, 0)),
            pl.BlockSpec((TILE, width), lambda t, *_: (t, 0)),
            pl.BlockSpec((NB, BLK, PW), lambda t, *_: (0, 0, 0)),
            pl.BlockSpec((NB, BLK, BLK), lambda t, *_: (0, 0, 0)),
        ],
        out_specs=[
            pl.BlockSpec((TILE, PW), lambda t, *_: (t, 0)),
            pl.BlockSpec((TILE, width), lambda t, *_: (t, 0)),
        ],
        scratch_shapes=[
            pltpu.VMEM((TILE, PW), jnp.bfloat16),
            pltpu.VMEM((TILE, PW), jnp.bfloat16),
            pltpu.VMEM((width, PW), jnp.bfloat16),
            pltpu.VMEM((width, PW), jnp.bfloat16),
            pltpu.VMEM((PW, PW), jnp.bfloat16),
            pltpu.VMEM((PW, PW), jnp.bfloat16),
        ],
    )
    return pl.pallas_call(
        tail_kernel,
        grid_spec=grid_spec,
        out_shape=[
            jax.ShapeDtypeStruct((rows, PW), jnp.float32),
            jax.ShapeDtypeStruct((rows, width), jnp.float32),
        ],
        compiler_params=pltpu.CompilerParams(vmem_limit_bytes=48 * 2**20),
        cost_estimate=pl.CostEstimate(
            flops=10 * 10**9, bytes_accessed=20 * 10**6, transcendentals=0
        ),
    )(at, pattern, panel_cols, partner_cols, matrix, work, diag)


def pack_kernel(at_ref, corner_ref, out_ref):
    row, odd = at_ref[0] % NB, at_ref[1] % 2
    for i in range(NB):
        for parity in range(2):

            @pl.when((row == i) & (odd == parity))
            def _():
                for slot in range(SLOTS):
                    held = HOLD[i][parity]
                    block = corner_ref[held[min(slot, len(held) - 1)] // 2]
                    for target in range(out_ref.shape[0]):
                        out_ref[target, slot] = block


def pack(at, corner, rows):
    return pl.pallas_call(
        pack_kernel,
        out_shape=jax.ShapeDtypeStruct((rows, SLOTS) + corner.shape[1:], jnp.float32),
        in_specs=[
            pl.BlockSpec(memory_space=pltpu.SMEM),
            pl.BlockSpec(memory_space=pltpu.VMEM),
        ],
        out_specs=pl.BlockSpec(memory_space=pltpu.VMEM),
        compiler_params=pltpu.CompilerParams(vmem_limit_bytes=16 * 2**20),
    )(at, corner)


def on_device(matrix, pattern):
    rows = lax.axis_size("row")
    cols = lax.axis_size("col")
    row = lax.axis_index("row")
    col = lax.axis_index("col")
    both = ("row", "col")

    def at(r, c):
        return r * cols + c

    def pairs(target, width=cols):
        return [(at(r, c), at(*target(r, c))) for r in range(rows) for c in range(width)]

    first = matrix[:, :BLK]
    cut = BLK // 2
    groups = [
        [at(r + o, c) for o in (0, NB) for c in range(core, cols, 2)]
        for r in range(NB)
        for core in range(2)
    ]
    corner = jnp.repeat(first[:BLK].reshape(2, cut, BLK), cols // 2, axis=0)
    corner = lax.all_to_all(corner, both, 0, 0, axis_index_groups=groups)
    first, corner = lax.optimization_barrier((first, corner))

    place = jnp.stack([row, col]).astype(jnp.int32)

    panel_cols = lax.all_gather(first, "col", axis=0)

    own = lax.all_to_all(pack(place, corner, rows), "row", 0, 0)
    first, own = lax.optimization_barrier((first, own))
    other = lax.ppermute(own, both, pairs(lambda r, c: (r, c ^ 1)))

    span = matrix.shape[1] // 2
    shares = [
        lax.ppermute(
            first[h * span : (h + 1) * span],
            both,
            pairs(lambda r, c, h=h: ((2 * c + h) ^ r, r), NB),
        )
        for h in range(2)
    ]
    odd = (col % 2).astype(jnp.int32).reshape(1)
    state = factor_call(start_kernel, (odd,), (own, other), {}, 3)
    shares, state = lax.optimization_barrier((shares, state))
    share = jnp.where((row ^ col) % 2 == 0, shares[0], shares[1])
    partner_cols = lax.all_to_all(
        jnp.broadcast_to(share[None], (rows,) + share.shape), "row", 0, 0
    )
    work, diag, _, _ = factor_call(finish_kernel, (), state, {i: i for i in range(4)}, 4)
    panel, schur = tail(place, pattern, panel_cols, partner_cols, matrix, work, diag)
    return (panel, schur)


def solution(mesh):
    in_specs = (P("row", "col"), P())
    out_specs = (P("row", None), P("row", "col"))
    return jax.shard_map(
        on_device, mesh=mesh, in_specs=in_specs, out_specs=out_specs, check_vma=False
    )
```

time: 225 us -> 165 us (0.73)
  blocking collectives: 47.1 us -> 23.1 us
  Pallas kernels: 89.5 us -> 65.7 us
  starting transfers between devices: 43.7 us -> 29.7 us
  between operations: 19.9 us -> 14.1 us
  local copies, waits for them, and re-layouts: 8.62 us -> 12.9 us
  waiting for transfers between devices: 14.7 us -> 17.5 us
    all_to_all x1, blocking collectives: 47.1 us -> 23.1 us  [on_device(): own = lax.all_to_all(pack(place, corner, rows), 'row', 0, 0)]
    pallas_call x1 -> x3, Pallas kernels: 67 us -> 43.2 us  [the longest x2 42.4 us: factor_call(): pl.pallas_call(kernel, out_shape=STATE, in_specs=[pl.BlockSpec(memory_spa...]
    all_to_all x1 -> x2, starting transfers between devices: 28.5 us -> 16.5 us  [the longest x1 11.6 us: on_device(): corner = lax.all_to_all(corner, both, 0, 0, axis_index_groups=groups)]
    all_to_all x1 -> x2, waiting for transfers between devices: 9.39 us -> 17.5 us  [the longest x1 13.3 us: on_device(): corner = lax.all_to_all(corner, both, 0, 0, axis_index_groups=groups)]
    unnamed x8 -> x12, local copies, waits for them, and re-layouts: 2.93 us -> 7.77 us
    ppermute x1, waiting for transfers between devices: 2.96 us -> 0.01 us  [on_device(): other = lax.ppermute(own, both, pairs(lambda r, c: (r, c ^ 1)))]
    ppermute x2, waiting for transfers between devices: 2.36 us -> 0.01 us  [on_device(): lax.ppermute(first[h * span:(h + 1) * span], both, pairs(lambda r, c, h=h...]
  transfers between devices with their start and end apart: 6 -> 6, of which waited for: 3 -> 2; matrix products, arithmetic and copies ran while one was open for 2% -> 2% of each run, Pallas kernels for 30% -> 26%
where the time goes in v3:
time: 165 us; the launch traced here: 163 us
  Pallas kernels  65.7 us (40%)
  starting transfers between devices  29.7 us (18%)
  blocking collectives  23.1 us (14%)
  waiting for transfers between devices  17.5 us (11%)
  between operations  14.1 us (9%)
  local copies, waits for them, and re-layouts  12.9 us (8%)
    pallas_call x2, Pallas kernels, factor_call(): pl.pallas_call(kernel, out_shape=STATE, in_specs=[pl.BlockSpec(memory_spa...  42.4 us
    all_to_all x1, blocking collectives, on_device(): own = lax.all_to_all(pack(place, corner, rows), 'row', 0, 0)  23.1 us
    pallas_call x1, Pallas kernels, tail(): pl.pallas_call(tail_kernel, grid_spec=grid_spec, out_shape=[jax.ShapeDtyp...  22.5 us
    all_to_all x1, waiting for transfers between devices, on_device(): corner = lax.all_to_all(corner, both, 0, 0, axis_index_groups=groups)  13.3 us
    all_to_all x1, starting transfers between devices, on_device(): corner = lax.all_to_all(corner, both, 0, 0, axis_index_groups=groups)  11.6 us
    ppermute x2, starting transfers between devices, on_device(): lax.ppermute(first[h * span:(h + 1) * span], both, pairs(lambda r, c, h=h...  8.37 us
    unnamed x12, local copies, waits for them, and re-layouts  7.77 us
    all_to_all x1, starting transfers between devices, on_device(): lax.all_to_all(jnp.broadcast_to(share[None], (rows,) + share.shape), 'row...  4.91 us
  transfers between devices with their start and end apart: 6, of which 2 were waited for; matrix products, arithmetic and copies ran while one was open for 2% of the time, Pallas kernels for 26%

profile of v3, /device:TPU:1, one launch (start us, length us, event | category | flops | bytes accessed | tf_op | source)
XLA Modules:
  0.0 163.2 jit_solution(17465455274405498994)
XLA Ops:
  7.2 0.8 slice.14
  8.0 0.8 broadcast_in_dim.4
  8.9 11.6 %all-to-all-start = ((f32[16,64,128]{2,1,0:T(8,128)}), f32[16,64,128]{2,1,0:T(8,128)S(1)}, u32[]{:S(2)}, u32[]{:S(2)}) async-start(f32[16,64,128]{2,1,0:T(8,128)} %bitcast.3), calls=%async_computation | async-start | bytes 1048576 | tf_op jit(solution)/shard_map/all_to_all | solution.py:372
  20.4 0.0 all-gather.3.cloned.1.call-start
  20.5 1.9 %slice.13 = f32[1024,128]{1,0:T(8,128)} slice(f32[1024,512]{1,0:T(8,128)} %m_ref.1), slice={[0:1024], [0:128]} | slice | bytes 1048576 | tf_op jit(solution)/shard_map/slice | solution.py:364
  22.4 13.3 %all-to-all-done.corner_ref = f32[16,64,128]{2,1,0:T(8,128)S(1)} async-done(((f32[16,64,128]{2,1,0:T(8,128)}), f32[16,64,128]{2,1,0:T(8,128)S(1)}, u32[]{:S(2)}, u32[]{:S(2)}) %all-to-all-start) | async-done | bytes 524320 | tf_op jit(solution)/shard_map/all_to_all | solution.py:372
  35.7 0.0 all-gather.3.cloned.1.call-update
  35.7 0.1 pad_add_fusion.at_ref
  35.8 0.8 shard_map.41
  36.6 0.0 copy-start.5
  36.6 23.1 %all_to_all.15.own_ref = f32[16,3,64,128]{3,2,1,0:T(8,128)S(1)} all-to-all(f32[16,3,64,128]{3,2,1,0:T(8,128)S(1)} %shard_map.41), channel_id=1, replica_groups=mesh['row'=16,'col'=16] {'row'}, dimensions={0} | all-to-all | bytes 3145728 | tf_op jit(solution)/shard_map/all_to_all | solution.py:379
  59.7 4.8 %collective-permute-start.2 = (f32[16,3,64,128]{3,2,1,0:T(8,128)S(1)}, f32[16,3,64,128]{3,2,1,0:T(8,128)}, u32[]{:S(2)}, u32[]{:S(2)}) collective-permute-start(f32[16,3,64,128]{3,2,1,0:T(8,128)S(1)} %all_to_all.15.own_ref), channel_id=1, source_target_pairs={{0,1},{1,0},{2,3},{3,2},{4,5},{5,4},{6,7},{7,6},{8,9},{9,8},{10,11... | collective-permute-start | bytes 4718600 | tf_op jit(solution)/shard_map/ppermute | solution.py:381
  64.5 0.0 copy-done.5
  64.5 2.1 %collective-permute-start.1 = (f32[256,128]{1,0:T(8,128)S(1)}, f32[256,128]{1,0:T(8,128)S(1)}, u32[]{:S(2)}, u32[]{:S(2)}) collective-permute-start(f32[256,128]{1,0:T(8,128)S(1)} %get-tuple-element.34), channel_id=1, source_target_pairs={{0,16},{1,48},{2,80},{3,112},{4,144},{5,176},{6,208},{7,240},{16,1... | collective-permute-start | bytes 393224 | tf_op jit(solution)/shard_map/ppermute | solution.py:385
  66.6 6.3 %collective-permute-start = (f32[256,128]{1,0:T(8,128)S(1)}, f32[256,128]{1,0:T(8,128)S(1)}, u32[]{:S(2)}, u32[]{:S(2)}) collective-permute-start(f32[256,128]{1,0:T(8,128)S(1)} %get-tuple-element.35), channel_id=1, source_target_pairs={{0,0},{1,32},{2,64},{3,96},{4,128},{5,160},{6,192},{7,224},{16,17}... | collective-permute-start | bytes 393224 | tf_op jit(solution)/shard_map/ppermute | solution.py:385
  72.9 0.0 collective-permute-done.2.other_ref
  72.9 21.7 %shard_map.42 = (f32[8,128,1024]{2,1,0:T(8,128)S(1)}, f32[8,128,128]{2,1,0:T(8,128)S(1)}, f32[128,128]{1,0:T(8,128)S(1)}, f32[128,128]{1,0:T(8,128)S(1)}) custom-call(s32[1]{0:T(128)} %bitcast.5.odd_ref, f32[16,3,64,128]{3,2,1,0:T(8,128)S(1)} %all_to_all.15.own_ref, f32[16,3,64,128]{3,2,1,0:T(8,128)} %collective-permute-done.2.other_ref), custom_call_target="tpu_custom_call" | custom-call | flops 30000001024 | bytes 75000000 | tf_op jit(solution)/shard_map/pallas_call | solution.py:189
  94.6 0.0 copy-start.2
  94.6 2.0 %copy-done.2 = f32[8,128,1024]{2,1,0:T(8,128)} copy-done((f32[8,128,1024]{2,1,0:T(8,128)}, f32[8,128,1024]{2,1,0:T(8,128)S(1)}, u32[]{:S(2)}) %copy-start.2) | copy-done | bytes 4194328
  96.6 0.0 collective-permute-done.1
  96.6 0.0 collective-permute-done
  96.7 1.5 broadcast_in_dim.10
  98.2 4.9 %all-to-all-start.2 = ((f32[16,256,128]{2,1,0:T(8,128)}), f32[16,256,128]{2,1,0:T(8,128)S(1)}, u32[]{:S(2)}, u32[]{:S(2)}) async-start(f32[16,256,128]{2,1,0:T(8,128)} %broadcast_in_dim.10), calls=%async_computation.2 | async-start | bytes 4194304 | tf_op jit(solution)/shard_map/all_to_all | solution.py:396
  103.1 0.0 copy-start.3
  103.1 2.2 %copy-done.3 = f32[8,128,1024]{2,1,0:T(8,128)S(1)} copy-done((f32[8,128,1024]{2,1,0:T(8,128)S(1)}, f32[8,128,1024]{2,1,0:T(8,128)}, u32[]{:S(2)}) %copy-start.3) | copy-done | bytes 4194328
  105.3 20.8 %shard_map.43 = (f32[8,128,1024]{2,1,0:T(8,128)S(1)}, f32[8,128,128]{2,1,0:T(8,128)S(1)}, f32[128,128]{1,0:T(8,128)S(1)}, f32[128,128]{1,0:T(8,128)S(1)}) custom-call(f32[8,128,1024]{2,1,0:T(8,128)S(1)} %copy-done.3, f32[8,128,128]{2,1,0:T(8,128)S(1)} %get-tuple-element.29.d_in, ...), custom_call_target="tpu_custom_call", output_to_operand_aliasing={{0}: (0, {}), {1}: (1, {}), {2}: (2, {}), {3}: (3, {})} | custom-call | flops 40000000000 | bytes 100000000 | tf_op jit(solution)/shard_map/pallas_call | solution.py:189
  126.1 0.0 copy-start.4
  126.1 2.0 %copy-done.4 = f32[8,128,1024]{2,1,0:T(8,128)} copy-done((f32[8,128,1024]{2,1,0:T(8,128)}, f32[8,128,1024]{2,1,0:T(8,128)S(1)}, u32[]{:S(2)}) %copy-start.4) | copy-done | bytes 4194328
  128.0 4.2 %all-to-all-done.2.wq_ref = f32[16,256,128]{2,1,0:T(8,128)S(1)} async-done(((f32[16,256,128]{2,1,0:T(8,128)}), f32[16,256,128]{2,1,0:T(8,128)S(1)}, u32[]{:S(2)}, u32[]{:S(2)}) %all-to-all-start.2) | async-done | bytes 2097184 | tf_op jit(solution)/shard_map/all_to_all | solution.py:396
  132.2 0.0 copy-done.1
  132.2 1.6 copy-done
  133.8 22.5 %shard_map.44 = (f32[1024,1024]{1,0:T(8,128)}, f32[1024,512]{1,0:T(8,128)}) custom-call(s32[2]{0:T(128)S(1)} %pad_add_fusion.at_ref, s32[2,128]{1,0:T(2,128)S(1)} %copy-done.1, f32[16,1024,128]{2,1,0:T(8,128)} %bitcast.7, f32[16,256,128]{2,1,0:T(8,128)S(1)} %all-to-all-done.2.wq_ref, f32[1024,512]{1,0:T(8,128)S(1)} %copy-done, f32[8,128,1024]{2,1,0:T(8,128)} %copy-done.4, ...), custom_call_target="tpu_custom_call" | custom-call | flops 10000000000 | bytes 20000000 | tf_op jit(solution)/shard_map/pallas_call | solution.py:310
  (5 shorter events, 0.0 us)
Async XLA Ops:
  8.9 26.8 %all-to-all-start = ((f32[16,64,128]{2,1,0:T(8,128)}), f32[16,64,128]{2,1,0:T(8,128)S(1)}, u32[]{:S(2)}, u32[]{:S(2)}) async-start(f32[16,64,128]{2,1,0:T(8,128)} %bitcast.3), calls=%async_computation | async-start | bytes 1048576 | tf_op jit(solution)/shard_map/all_to_all | solution.py:372
  20.4 111.8 %all-gather.3.cloned.1.call-start = ((), (), s32[]{:S(2)}) async-start(), calls=%async_computation.3 | async-start | bytes 8912896 | tf_op jit(solution)/shard_map/all_gather | solution.py:377
  36.6 28.0 %copy-start.5 = (f32[1024,128]{1,0:T(8,128)S(1)}, f32[1024,128]{1,0:T(8,128)}, u32[]{:S(2)}) copy-start(f32[1024,128]{1,0:T(8,128)} %slice.13) | copy-start | bytes 1572868
  59.7 13.2 %collective-permute-start.2 = (f32[16,3,64,128]{3,2,1,0:T(8,128)S(1)}, f32[16,3,64,128]{3,2,1,0:T(8,128)}, u32[]{:S(2)}, u32[]{:S(2)}) collective-permute-start(f32[16,3,64,128]{3,2,1,0:T(8,128)S(1)} %all_to_all.15.own_ref), channel_id=1, source_target_pairs={{0,1},{1,0},{2,3},{3,2},{4,5},{5,4},{6,7},{7,6},{8,9},{9,8},{10,11... | collective-permute-start | bytes 4718600 | tf_op jit(solution)/shard_map/ppermute | solution.py:381
  64.5 32.1 %collective-permute-start.1 = (f32[256,128]{1,0:T(8,128)S(1)}, f32[256,128]{1,0:T(8,128)S(1)}, u32[]{:S(2)}, u32[]{:S(2)}) collective-permute-start(f32[256,128]{1,0:T(8,128)S(1)} %get-tuple-element.34), channel_id=1, source_target_pairs={{0,16},{1,48},{2,80},{3,112},{4,144},{5,176},{6,208},{7,240},{16,1... | collective-permute-start | bytes 393224 | tf_op jit(solution)/shard_map/ppermute | solution.py:385
  66.6 30.0 %collective-permute-start = (f32[256,128]{1,0:T(8,128)S(1)}, f32[256,128]{1,0:T(8,128)S(1)}, u32[]{:S(2)}, u32[]{:S(2)}) collective-permute-start(f32[256,128]{1,0:T(8,128)S(1)} %get-tuple-element.35), channel_id=1, source_target_pairs={{0,0},{1,32},{2,64},{3,96},{4,128},{5,160},{6,192},{7,224},{16,17}... | collective-permute-start | bytes 393224 | tf_op jit(solution)/shard_map/ppermute | solution.py:385
  94.6 2.0 %copy-start.2 = (f32[8,128,1024]{2,1,0:T(8,128)}, f32[8,128,1024]{2,1,0:T(8,128)S(1)}, u32[]{:S(2)}) copy-start(f32[8,128,1024]{2,1,0:T(8,128)S(1)} %get-tuple-element.28.w_in) | copy-start | bytes 12582916
  98.2 34.0 %all-to-all-start.2 = ((f32[16,256,128]{2,1,0:T(8,128)}), f32[16,256,128]{2,1,0:T(8,128)S(1)}, u32[]{:S(2)}, u32[]{:S(2)}) async-start(f32[16,256,128]{2,1,0:T(8,128)} %broadcast_in_dim.10), calls=%async_computation.2 | async-start | bytes 4194304 | tf_op jit(solution)/shard_map/all_to_all | solution.py:396
  103.1 2.2 %copy-start.3 = (f32[8,128,1024]{2,1,0:T(8,128)S(1)}, f32[8,128,1024]{2,1,0:T(8,128)}, u32[]{:S(2)}) copy-start(f32[8,128,1024]{2,1,0:T(8,128)} %copy-done.2) | copy-start | bytes 12582916
  105.3 26.9 %copy-start.1 = (s32[2,128]{1,0:T(2,128)S(1)}, s32[2,128]{1,0:T(2,128)}, u32[]{:S(2)}) copy-start(s32[2,128]{1,0:T(2,128)} %pattern_ref.1) | copy-start | bytes 3076
  126.1 2.0 %copy-start.4 = (f32[8,128,1024]{2,1,0:T(8,128)}, f32[8,128,1024]{2,1,0:T(8,128)S(1)}, u32[]{:S(2)}) copy-start(f32[8,128,1024]{2,1,0:T(8,128)S(1)} %get-tuple-element.32.work) | copy-start | bytes 12582916
  132.2 1.6 copy-start
Sparse Core Ops, SparseCore 0:
  35.8 70.0 all-gather.2

commit v4 on v3

--- a/solution.py
+++ b/solution.py
@@ -192,7 +192,7 @@
         in_specs=[pl.BlockSpec(memory_space=pltpu.SMEM)] * len(scalars) + [vmem] * len(operands),
         out_specs=[vmem] * len(STATE),
         input_output_aliases=aliases,
-        compiler_params=pltpu.CompilerParams(vmem_limit_bytes=32 * 2**20),
+        compiler_params=pltpu.CompilerParams(vmem_limit_bytes=24 * 2**20),
         cost_estimate=pl.CostEstimate(
             flops=share * 10**10, bytes_accessed=share * 25 * 10**6, transcendentals=0
         ),
@@ -200,13 +200,12 @@
 
 
 def dot3(a, b):
-    def term(x, y):
-        return lax.dot_general(x, y, (((1,), (1,)), ((), ())), preferred_element_type=jnp.float32)
-
-    return term(a[0], b[0]) + (term(a[0], b[1]) + term(a[1], b[0]))
-
-
-TILE = 256
+    return dot_nt(
+        jnp.concatenate([a[0], a[1], a[0]], axis=1), jnp.concatenate([b[0], b[0], b[1]], axis=1)
+    )
+
+
+TILE = 512
 STEP = 256
 
 
@@ -243,7 +242,9 @@
                     j,
                     per * h,
                     col,
-                    lambda j, b: wq_ref[(2 * j + h) ^ col, b * BLK : (b + 1) * BLK, :],
+                    lambda j, b: wq_ref[
+                        (2 * j + (per * h + b) // 2) ^ col, b % 2 * BLK : (b % 2 + 1) * BLK, :
+                    ],
                 )
 
             def keep(cols, value):
@@ -283,16 +284,15 @@
 
 def tail(at, pattern, panel_cols, partner_cols, matrix, work, diag):
     rows, width = matrix.shape
-    pieces = partner_cols.shape
     grid_spec = pltpu.PrefetchScalarGridSpec(
         num_scalar_prefetch=2,
         grid=(rows // TILE,),
         in_specs=[
             pl.BlockSpec((NB, TILE, BLK), lambda t, *_: (0, t, 0)),
-            pl.BlockSpec(pieces, lambda t, *_: (0, 0, 0)),
+            pl.BlockSpec(memory_space=pltpu.VMEM),
             pl.BlockSpec((TILE, width), lambda t, *_: (t, 0)),
-            pl.BlockSpec((NB, BLK, PW), lambda t, *_: (0, 0, 0)),
-            pl.BlockSpec((NB, BLK, BLK), lambda t, *_: (0, 0, 0)),
+            pl.BlockSpec(memory_space=pltpu.VMEM),
+            pl.BlockSpec(memory_space=pltpu.VMEM),
         ],
         out_specs=[
             pl.BlockSpec((TILE, PW), lambda t, *_: (t, 0)),
@@ -314,7 +314,7 @@
             jax.ShapeDtypeStruct((rows, PW), jnp.float32),
             jax.ShapeDtypeStruct((rows, width), jnp.float32),
         ],
-        compiler_params=pltpu.CompilerParams(vmem_limit_bytes=48 * 2**20),
+        compiler_params=pltpu.CompilerParams(vmem_limit_bytes=44 * 2**20),
         cost_estimate=pl.CostEstimate(
             flops=10 * 10**9, bytes_accessed=20 * 10**6, transcendentals=0
         ),

time: 165 us -> 159 us (0.964)
  Pallas kernels: 65.7 us -> 57.8 us
  local copies, waits for them, and re-layouts: 12.9 us -> 15.1 us
    pallas_call x1, Pallas kernels: 22.5 us -> 14.6 us  [tail(): pl.pallas_call(tail_kernel, grid_spec=grid_spec, out_shape=[jax.ShapeDtyp...]
    unnamed x12 -> x14, local copies, waits for them, and re-layouts: 7.77 us -> 10 us
  transfers between devices with their start and end apart: 6 -> 6, of which waited for: 2 -> 2; matrix products, arithmetic and copies ran while one was open for 2% -> 2% of each run, Pallas kernels for 26% -> 27%
where the time goes in v4:
time: 159 us; the launch traced here: 157 us
  Pallas kernels  57.8 us (36%)
  starting transfers between devices  29.7 us (19%)
  blocking collectives  23.1 us (15%)
  waiting for transfers between devices  17.5 us (11%)
  local copies, waits for them, and re-layouts  15.1 us (9%)
  between operations  14.1 us (9%)
    pallas_call x2, Pallas kernels, factor_call(): pl.pallas_call(kernel, out_shape=STATE, in_specs=[pl.BlockSpec(memory_spa...  42.4 us
    all_to_all x1, blocking collectives, on_device(): own = lax.all_to_all(pack(place, corner, rows), 'row', 0, 0)  23.1 us
    pallas_call x1, Pallas kernels, tail(): pl.pallas_call(tail_kernel, grid_spec=grid_spec, out_shape=[jax.ShapeDtyp...  14.6 us
    all_to_all x1, waiting for transfers between devices, on_device(): corner = lax.all_to_all(corner, both, 0, 0, axis_index_groups=groups)  13.3 us
    all_to_all x1, starting transfers between devices, on_device(): corner = lax.all_to_all(corner, both, 0, 0, axis_index_groups=groups)  11.6 us
    unnamed x14, local copies, waits for them, and re-layouts  10 us
    ppermute x2, starting transfers between devices, on_device(): lax.ppermute(first[h * span:(h + 1) * span], both, pairs(lambda r, c, h=h...  8.37 us
    all_to_all x1, starting transfers between devices, on_device(): lax.all_to_all(jnp.broadcast_to(share[None], (rows,) + share.shape), 'row...  4.91 us
  transfers between devices with their start and end apart: 6, of which 2 were waited for; matrix products, arithmetic and copies ran while one was open for 2% of the time, Pallas kernels for 27%

profile of v4, /device:TPU:1, one launch (start us, length us, event | category | flops | bytes accessed | tf_op | source)
XLA Modules:
  0.0 157.5 jit_solution(14437067258475226633)
XLA Ops:
  7.2 0.8 slice.14
  8.0 0.8 broadcast_in_dim.4
  8.9 11.6 %all-to-all-start = ((f32[16,64,128]{2,1,0:T(8,128)}), f32[16,64,128]{2,1,0:T(8,128)S(1)}, u32[]{:S(2)}, u32[]{:S(2)}) async-start(f32[16,64,128]{2,1,0:T(8,128)} %bitcast.3), calls=%async_computation | async-start | bytes 1048576 | tf_op jit(solution)/shard_map/all_to_all | solution.py:372
  20.4 0.0 all-gather.3.cloned.1.call-start
  20.5 1.9 %slice.13 = f32[1024,128]{1,0:T(8,128)} slice(f32[1024,512]{1,0:T(8,128)} %m_ref.1), slice={[0:1024], [0:128]} | slice | bytes 1048576 | tf_op jit(solution)/shard_map/slice | solution.py:364
  22.4 13.3 %all-to-all-done.corner_ref = f32[16,64,128]{2,1,0:T(8,128)S(1)} async-done(((f32[16,64,128]{2,1,0:T(8,128)}), f32[16,64,128]{2,1,0:T(8,128)S(1)}, u32[]{:S(2)}, u32[]{:S(2)}) %all-to-all-start) | async-done | bytes 524320 | tf_op jit(solution)/shard_map/all_to_all | solution.py:372
  35.7 0.0 all-gather.3.cloned.1.call-update
  35.7 0.1 pad_add_fusion.at_ref
  35.8 0.8 shard_map.41
  36.6 0.0 copy-start.6
  36.6 23.1 %all_to_all.15.own_ref = f32[16,3,64,128]{3,2,1,0:T(8,128)S(1)} all-to-all(f32[16,3,64,128]{3,2,1,0:T(8,128)S(1)} %shard_map.41), channel_id=1, replica_groups=mesh['row'=16,'col'=16] {'row'}, dimensions={0} | all-to-all | bytes 3145728 | tf_op jit(solution)/shard_map/all_to_all | solution.py:379
  59.7 4.8 %collective-permute-start.2 = (f32[16,3,64,128]{3,2,1,0:T(8,128)S(1)}, f32[16,3,64,128]{3,2,1,0:T(8,128)}, u32[]{:S(2)}, u32[]{:S(2)}) collective-permute-start(f32[16,3,64,128]{3,2,1,0:T(8,128)S(1)} %all_to_all.15.own_ref), channel_id=1, source_target_pairs={{0,1},{1,0},{2,3},{3,2},{4,5},{5,4},{6,7},{7,6},{8,9},{9,8},{10,11... | collective-permute-start | bytes 4718600 | tf_op jit(solution)/shard_map/ppermute | solution.py:381
  64.5 0.0 copy-done.6
  64.5 2.1 %collective-permute-start.1 = (f32[256,128]{1,0:T(8,128)S(1)}, f32[256,128]{1,0:T(8,128)S(1)}, u32[]{:S(2)}, u32[]{:S(2)}) collective-permute-start(f32[256,128]{1,0:T(8,128)S(1)} %get-tuple-element.34), channel_id=1, source_target_pairs={{0,16},{1,48},{2,80},{3,112},{4,144},{5,176},{6,208},{7,240},{16,1... | collective-permute-start | bytes 393224 | tf_op jit(solution)/shard_map/ppermute | solution.py:385
  66.6 6.3 %collective-permute-start = (f32[256,128]{1,0:T(8,128)S(1)}, f32[256,128]{1,0:T(8,128)S(1)}, u32[]{:S(2)}, u32[]{:S(2)}) collective-permute-start(f32[256,128]{1,0:T(8,128)S(1)} %get-tuple-element.35), channel_id=1, source_target_pairs={{0,0},{1,32},{2,64},{3,96},{4,128},{5,160},{6,192},{7,224},{16,17}... | collective-permute-start | bytes 393224 | tf_op jit(solution)/shard_map/ppermute | solution.py:385
  72.9 0.0 collective-permute-done.2.other_ref
  72.9 21.7 %shard_map.42 = (f32[8,128,1024]{2,1,0:T(8,128)S(1)}, f32[8,128,128]{2,1,0:T(8,128)S(1)}, f32[128,128]{1,0:T(8,128)S(1)}, f32[128,128]{1,0:T(8,128)S(1)}) custom-call(s32[1]{0:T(128)} %bitcast.5.odd_ref, f32[16,3,64,128]{3,2,1,0:T(8,128)S(1)} %all_to_all.15.own_ref, f32[16,3,64,128]{3,2,1,0:T(8,128)} %collective-permute-done.2.other_ref), custom_call_target="tpu_custom_call" | custom-call | flops 30000001024 | bytes 75000000 | tf_op jit(solution)/shard_map/pallas_call | solution.py:189
  94.6 0.0 copy-start.2
  94.6 2.0 %copy-done.2 = f32[8,128,1024]{2,1,0:T(8,128)} copy-done((f32[8,128,1024]{2,1,0:T(8,128)}, f32[8,128,1024]{2,1,0:T(8,128)S(1)}, u32[]{:S(2)}) %copy-start.2) | copy-done | bytes 4194328
  96.6 0.0 collective-permute-done.1
  96.6 0.0 collective-permute-done
  96.7 1.5 broadcast_in_dim.10
  98.2 4.9 %all-to-all-start.2 = ((f32[16,256,128]{2,1,0:T(8,128)}), f32[16,256,128]{2,1,0:T(8,128)S(1)}, u32[]{:S(2)}, u32[]{:S(2)}) async-start(f32[16,256,128]{2,1,0:T(8,128)} %broadcast_in_dim.10), calls=%async_computation.2 | async-start | bytes 4194304 | tf_op jit(solution)/shard_map/all_to_all | solution.py:396
  103.1 0.0 copy-start.3
  103.1 2.2 %copy-done.3 = f32[8,128,1024]{2,1,0:T(8,128)S(1)} copy-done((f32[8,128,1024]{2,1,0:T(8,128)S(1)}, f32[8,128,1024]{2,1,0:T(8,128)}, u32[]{:S(2)}) %copy-start.3) | copy-done | bytes 4194328
  105.3 20.8 %shard_map.43 = (f32[8,128,1024]{2,1,0:T(8,128)S(1)}, f32[8,128,128]{2,1,0:T(8,128)S(1)}, f32[128,128]{1,0:T(8,128)S(1)}, f32[128,128]{1,0:T(8,128)S(1)}) custom-call(f32[8,128,1024]{2,1,0:T(8,128)S(1)} %copy-done.3, f32[8,128,128]{2,1,0:T(8,128)S(1)} %get-tuple-element.29.d_in, ...), custom_call_target="tpu_custom_call", output_to_operand_aliasing={{0}: (0, {}), {1}: (1, {}), {2}: (2, {}), {3}: (3, {})} | custom-call | flops 40000000000 | bytes 100000000 | tf_op jit(solution)/shard_map/pallas_call | solution.py:189
  126.1 0.0 copy-start.4
  126.1 2.0 %copy-done.4 = f32[8,128,1024]{2,1,0:T(8,128)} copy-done((f32[8,128,1024]{2,1,0:T(8,128)}, f32[8,128,1024]{2,1,0:T(8,128)S(1)}, u32[]{:S(2)}) %copy-start.4) | copy-done | bytes 4194328
  128.1 4.1 %all-to-all-done.2.wq_ref = f32[16,256,128]{2,1,0:T(8,128)S(1)} async-done(((f32[16,256,128]{2,1,0:T(8,128)}), f32[16,256,128]{2,1,0:T(8,128)S(1)}, u32[]{:S(2)}, u32[]{:S(2)}) %all-to-all-start.2) | async-done | bytes 2097184 | tf_op jit(solution)/shard_map/all_to_all | solution.py:396
  132.2 1.6 %copy-done = f32[1024,512]{1,0:T(8,128)S(1)} copy-done((f32[1024,512]{1,0:T(8,128)S(1)}, f32[1024,512]{1,0:T(8,128)}, u32[]{:S(2)}) %copy-start) | copy-done | bytes 2097176
  133.8 2.2 %copy-done.5 = f32[8,128,1024]{2,1,0:T(8,128)S(1)} copy-done((f32[8,128,1024]{2,1,0:T(8,128)S(1)}, f32[8,128,1024]{2,1,0:T(8,128)}, u32[]{:S(2)}) %copy-start.5) | copy-done | bytes 4194328
  136.0 14.6 %shard_map.44 = (f32[1024,1024]{1,0:T(8,128)}, f32[1024,512]{1,0:T(8,128)}) custom-call(s32[2]{0:T(128)S(1)} %pad_add_fusion.at_ref, s32[2,128]{1,0:T(2,128)S(1)} %copy-done.1, f32[16,1024,128]{2,1,0:T(8,128)} %bitcast.7, f32[16,256,128]{2,1,0:T(8,128)S(1)} %all-to-all-done.2.wq_ref, f32[1024,512]{1,0:T(8,128)S(1)} %copy-done, ...), custom_call_target="tpu_custom_call" | custom-call | flops 10000000000 | bytes 20000000 | tf_op jit(solution)/shard_map/pallas_call | solution.py:310
  (7 shorter events, 0.0 us)
Async XLA Ops:
  8.9 26.8 %all-to-all-start = ((f32[16,64,128]{2,1,0:T(8,128)}), f32[16,64,128]{2,1,0:T(8,128)S(1)}, u32[]{:S(2)}, u32[]{:S(2)}) async-start(f32[16,64,128]{2,1,0:T(8,128)} %bitcast.3), calls=%async_computation | async-start | bytes 1048576 | tf_op jit(solution)/shard_map/all_to_all | solution.py:372
  20.4 111.8 %all-gather.3.cloned.1.call-start = ((), (), s32[]{:S(2)}) async-start(), calls=%async_computation.3 | async-start | bytes 8912896 | tf_op jit(solution)/shard_map/all_gather | solution.py:377
  36.6 28.0 %copy-start.6 = (f32[1024,128]{1,0:T(8,128)S(1)}, f32[1024,128]{1,0:T(8,128)}, u32[]{:S(2)}) copy-start(f32[1024,128]{1,0:T(8,128)} %slice.13) | copy-start | bytes 1572868
  59.7 13.2 %collective-permute-start.2 = (f32[16,3,64,128]{3,2,1,0:T(8,128)S(1)}, f32[16,3,64,128]{3,2,1,0:T(8,128)}, u32[]{:S(2)}, u32[]{:S(2)}) collective-permute-start(f32[16,3,64,128]{3,2,1,0:T(8,128)S(1)} %all_to_all.15.own_ref), channel_id=1, source_target_pairs={{0,1},{1,0},{2,3},{3,2},{4,5},{5,4},{6,7},{7,6},{8,9},{9,8},{10,11... | collective-permute-start | bytes 4718600 | tf_op jit(solution)/shard_map/ppermute | solution.py:381
  64.5 32.1 %collective-permute-start.1 = (f32[256,128]{1,0:T(8,128)S(1)}, f32[256,128]{1,0:T(8,128)S(1)}, u32[]{:S(2)}, u32[]{:S(2)}) collective-permute-start(f32[256,128]{1,0:T(8,128)S(1)} %get-tuple-element.34), channel_id=1, source_target_pairs={{0,16},{1,48},{2,80},{3,112},{4,144},{5,176},{6,208},{7,240},{16,1... | collective-permute-start | bytes 393224 | tf_op jit(solution)/shard_map/ppermute | solution.py:385
  66.6 30.0 %collective-permute-start = (f32[256,128]{1,0:T(8,128)S(1)}, f32[256,128]{1,0:T(8,128)S(1)}, u32[]{:S(2)}, u32[]{:S(2)}) collective-permute-start(f32[256,128]{1,0:T(8,128)S(1)} %get-tuple-element.35), channel_id=1, source_target_pairs={{0,0},{1,32},{2,64},{3,96},{4,128},{5,160},{6,192},{7,224},{16,17}... | collective-permute-start | bytes 393224 | tf_op jit(solution)/shard_map/ppermute | solution.py:385
  94.6 2.0 %copy-start.2 = (f32[8,128,1024]{2,1,0:T(8,128)}, f32[8,128,1024]{2,1,0:T(8,128)S(1)}, u32[]{:S(2)}) copy-start(f32[8,128,1024]{2,1,0:T(8,128)S(1)} %get-tuple-element.28.w_in) | copy-start | bytes 12582916
  98.2 34.0 %all-to-all-start.2 = ((f32[16,256,128]{2,1,0:T(8,128)}), f32[16,256,128]{2,1,0:T(8,128)S(1)}, u32[]{:S(2)}, u32[]{:S(2)}) async-start(f32[16,256,128]{2,1,0:T(8,128)} %broadcast_in_dim.10), calls=%async_computation.2 | async-start | bytes 4194304 | tf_op jit(solution)/shard_map/all_to_all | solution.py:396
  103.1 2.2 %copy-start.3 = (f32[8,128,1024]{2,1,0:T(8,128)S(1)}, f32[8,128,1024]{2,1,0:T(8,128)}, u32[]{:S(2)}) copy-start(f32[8,128,1024]{2,1,0:T(8,128)} %copy-done.2) | copy-start | bytes 12582916
  105.3 26.9 %copy-start.1 = (s32[2,128]{1,0:T(2,128)S(1)}, s32[2,128]{1,0:T(2,128)}, u32[]{:S(2)}) copy-start(s32[2,128]{1,0:T(2,128)} %pattern_ref.1) | copy-start | bytes 3076
  126.1 2.0 %copy-start.4 = (f32[8,128,1024]{2,1,0:T(8,128)}, f32[8,128,1024]{2,1,0:T(8,128)S(1)}, u32[]{:S(2)}) copy-start(f32[8,128,1024]{2,1,0:T(8,128)S(1)} %get-tuple-element.32.work) | copy-start | bytes 12582916
  132.2 1.6 %copy-start = (f32[1024,512]{1,0:T(8,128)S(1)}, f32[1024,512]{1,0:T(8,128)}, u32[]{:S(2)}) copy-start(f32[1024,512]{1,0:T(8,128)} %m_ref.1) | copy-start | bytes 6291460
  133.8 2.2 %copy-start.5 = (f32[8,128,1024]{2,1,0:T(8,128)S(1)}, f32[8,128,1024]{2,1,0:T(8,128)}, u32[]{:S(2)}) copy-start(f32[8,128,1024]{2,1,0:T(8,128)} %copy-done.4) | copy-start | bytes 12582916
Sparse Core Ops, SparseCore 0:
  35.8 70.0 all-gather.2

commit v5 on v4

--- a/solution.py
+++ b/solution.py
@@ -77,7 +77,6 @@
         rows = jnp.where(inside, jnp.where(lane == sub + c0, 1.0, 0.0), tiles[panel])
         upper = rows
         pivots = jnp.ones((8, BLK), jnp.float32)
-        below = {(g, k): lane_copy(tiles[g], c0 + k) for g in range(panel + 1, 16) for k in range(8)}
         for p in range(0, 8, 2):
             one, two = sub == p, sub == p + 1
             pair = one | two
@@ -101,7 +100,7 @@
         if panel < 15:
             solved = [row_copy(rows, k) for k in range(8)]
             for g in range(panel + 1, 16):
-                parts = [below[g, k] * solved[k] for k in range(8)]
+                parts = [lane_copy(tiles[g], c0 + k) * solved[k] for k in range(8)]
                 while len(parts) > 1:
                     parts = [parts[m] + parts[m + 1] for m in range(0, len(parts), 2)]
                 tiles[g] = jnp.where(inside, 0.0, tiles[g]) - parts[0]
@@ -134,7 +133,7 @@
         work[k] = dot_nn(inv_left, right6(work[k], 0))
         work[k, :, here] = inv
         sweep = right6(work[k], 0)
-        for i in range(1, NB):
+        for i in range(first + 1, NB):
             block = work[i, :, here]
             below = left6(jnp.where(i > k, dot_nt(left6(block), inv_right), 0.0))
             work[i, :, here] = jnp.where(i > k, 0.0, block)
@@ -146,7 +145,7 @@
     lax.fori_loop(first, last, step, 0)
 
 
-FIRST_STEPS = 3
+FIRST_STEPS = 2
 
 
 def start_kernel(odd_ref, own_ref, other_ref, work, diag, head, base):

time: 159 us -> 158 us (level)
  starting transfers between devices: 29.7 us -> 35.4 us
  waiting for transfers between devices: 17.5 us -> 13.6 us
  Pallas kernels: 57.8 us -> 55.9 us
    all_to_all x1, starting transfers between devices: 4.91 us -> 10.7 us  [on_device(): lax.all_to_all(jnp.broadcast_to(share[None], (rows,) + share.shape), 'row...]
    all_to_all x1, waiting for transfers between devices: 4.13 us -> 0.25 us  [on_device(): lax.all_to_all(jnp.broadcast_to(share[None], (rows,) + share.shape), 'row...]
    pallas_call x2, Pallas kernels: 42.4 us -> 40.6 us  [factor_call(): pl.pallas_call(kernel, out_shape=STATE, in_specs=[pl.BlockSpec(memory_spa...]
  transfers between devices with their start and end apart: 6 -> 6, of which waited for: 2 -> 2; matrix products, arithmetic and copies ran while one was open for 2% -> 2% of each run, Pallas kernels for 27% -> 26%
where the time goes in v5:
time: 158 us; the launch traced here: 157 us
  Pallas kernels  55.9 us (35%)
  starting transfers between devices  35.4 us (22%)
  blocking collectives  23.1 us (15%)
  local copies, waits for them, and re-layouts  15.1 us (10%)
  between operations  14.1 us (9%)
  waiting for transfers between devices  13.6 us (9%)
    pallas_call x2, Pallas kernels, factor_call(): pl.pallas_call(kernel, out_shape=STATE, in_specs=[pl.BlockSpec(memory_spa...  40.6 us
    all_to_all x1, blocking collectives, on_device(): own = lax.all_to_all(pack(place, corner, rows), 'row', 0, 0)  23.1 us
    pallas_call x1, Pallas kernels, tail(): pl.pallas_call(tail_kernel, grid_spec=grid_spec, out_shape=[jax.ShapeDtyp...  14.6 us
    all_to_all x1, waiting for transfers between devices, on_device(): corner = lax.all_to_all(corner, both, 0, 0, axis_index_groups=groups)  13.3 us
    all_to_all x1, starting transfers between devices, on_device(): corner = lax.all_to_all(corner, both, 0, 0, axis_index_groups=groups)  11.6 us
    all_to_all x1, starting transfers between devices, on_device(): lax.all_to_all(jnp.broadcast_to(share[None], (rows,) + share.shape), 'row...  10.7 us
    unnamed x14, local copies, waits for them, and re-layouts  10 us
    ppermute x2, starting transfers between devices, on_device(): lax.ppermute(first[h * span:(h + 1) * span], both, pairs(lambda r, c, h=h...  8.37 us
  transfers between devices with their start and end apart: 6, of which 2 were waited for; matrix products, arithmetic and copies ran while one was open for 2% of the time, Pallas kernels for 26%

profile of v5, /device:TPU:1, one launch (start us, length us, event | category | flops | bytes accessed | tf_op | source)
XLA Modules:
  0.0 157.5 jit_solution(12994162579939198078)
XLA Ops:
  7.2 0.8 slice.14
  8.0 0.8 broadcast_in_dim.4
  8.9 11.6 %all-to-all-start = ((f32[16,64,128]{2,1,0:T(8,128)}), f32[16,64,128]{2,1,0:T(8,128)S(1)}, u32[]{:S(2)}, u32[]{:S(2)}) async-start(f32[16,64,128]{2,1,0:T(8,128)} %bitcast.3), calls=%async_computation | async-start | bytes 1048576 | tf_op jit(solution)/shard_map/all_to_all | solution.py:371
  20.4 0.0 all-gather.3.cloned.1.call-start
  20.5 1.9 %slice.13 = f32[1024,128]{1,0:T(8,128)} slice(f32[1024,512]{1,0:T(8,128)} %m_ref.1), slice={[0:1024], [0:128]} | slice | bytes 1048576 | tf_op jit(solution)/shard_map/slice | solution.py:363
  22.4 13.3 %all-to-all-done.corner_ref = f32[16,64,128]{2,1,0:T(8,128)S(1)} async-done(((f32[16,64,128]{2,1,0:T(8,128)}), f32[16,64,128]{2,1,0:T(8,128)S(1)}, u32[]{:S(2)}, u32[]{:S(2)}) %all-to-all-start) | async-done | bytes 524320 | tf_op jit(solution)/shard_map/all_to_all | solution.py:371
  35.7 0.0 all-gather.3.cloned.1.call-update
  35.7 0.1 pad_add_fusion.at_ref
  35.8 0.8 shard_map.41
  36.6 0.0 copy-start.6
  36.6 23.1 %all_to_all.15.own_ref = f32[16,3,64,128]{3,2,1,0:T(8,128)S(1)} all-to-all(f32[16,3,64,128]{3,2,1,0:T(8,128)S(1)} %shard_map.41), channel_id=1, replica_groups=mesh['row'=16,'col'=16] {'row'}, dimensions={0} | all-to-all | bytes 3145728 | tf_op jit(solution)/shard_map/all_to_all | solution.py:378
  59.7 4.8 %collective-permute-start.2 = (f32[16,3,64,128]{3,2,1,0:T(8,128)S(1)}, f32[16,3,64,128]{3,2,1,0:T(8,128)}, u32[]{:S(2)}, u32[]{:S(2)}) collective-permute-start(f32[16,3,64,128]{3,2,1,0:T(8,128)S(1)} %all_to_all.15.own_ref), channel_id=1, source_target_pairs={{0,1},{1,0},{2,3},{3,2},{4,5},{5,4},{6,7},{7,6},{8,9},{9,8},{10,11... | collective-permute-start | bytes 4718600 | tf_op jit(solution)/shard_map/ppermute | solution.py:380
  64.5 0.0 copy-done.6
  64.5 2.1 %collective-permute-start.1 = (f32[256,128]{1,0:T(8,128)S(1)}, f32[256,128]{1,0:T(8,128)S(1)}, u32[]{:S(2)}, u32[]{:S(2)}) collective-permute-start(f32[256,128]{1,0:T(8,128)S(1)} %get-tuple-element.34), channel_id=1, source_target_pairs={{0,16},{1,48},{2,80},{3,112},{4,144},{5,176},{6,208},{7,240},{16,1... | collective-permute-start | bytes 393224 | tf_op jit(solution)/shard_map/ppermute | solution.py:384
  66.6 6.3 %collective-permute-start = (f32[256,128]{1,0:T(8,128)S(1)}, f32[256,128]{1,0:T(8,128)S(1)}, u32[]{:S(2)}, u32[]{:S(2)}) collective-permute-start(f32[256,128]{1,0:T(8,128)S(1)} %get-tuple-element.35), channel_id=1, source_target_pairs={{0,0},{1,32},{2,64},{3,96},{4,128},{5,160},{6,192},{7,224},{16,17}... | collective-permute-start | bytes 393224 | tf_op jit(solution)/shard_map/ppermute | solution.py:384
  72.9 0.0 collective-permute-done.2.other_ref
  72.9 15.9 %shard_map.42 = (f32[8,128,1024]{2,1,0:T(8,128)S(1)}, f32[8,128,128]{2,1,0:T(8,128)S(1)}, f32[128,128]{1,0:T(8,128)S(1)}, f32[128,128]{1,0:T(8,128)S(1)}) custom-call(s32[1]{0:T(128)} %bitcast.5.odd_ref, f32[16,3,64,128]{3,2,1,0:T(8,128)S(1)} %all_to_all.15.own_ref, f32[16,3,64,128]{3,2,1,0:T(8,128)} %collective-permute-done.2.other_ref), custom_call_target="tpu_custom_call" | custom-call | flops 30000001024 | bytes 75000000 | tf_op jit(solution)/shard_map/pallas_call | solution.py:188
  88.9 0.0 copy-start.2
  88.9 2.0 %copy-done.2 = f32[8,128,1024]{2,1,0:T(8,128)} copy-done((f32[8,128,1024]{2,1,0:T(8,128)}, f32[8,128,1024]{2,1,0:T(8,128)S(1)}, u32[]{:S(2)}) %copy-start.2) | copy-done | bytes 4194328
  90.9 0.0 collective-permute-done.1
  90.9 0.0 collective-permute-done
  90.9 1.5 broadcast_in_dim.10
  92.4 10.7 %all-to-all-start.2 = ((f32[16,256,128]{2,1,0:T(8,128)}), f32[16,256,128]{2,1,0:T(8,128)S(1)}, u32[]{:S(2)}, u32[]{:S(2)}) async-start(f32[16,256,128]{2,1,0:T(8,128)} %broadcast_in_dim.10), calls=%async_computation.2 | async-start | bytes 4194304 | tf_op jit(solution)/shard_map/all_to_all | solution.py:395
  103.1 0.0 copy-start.3
  103.1 2.2 %copy-done.3 = f32[8,128,1024]{2,1,0:T(8,128)S(1)} copy-done((f32[8,128,1024]{2,1,0:T(8,128)S(1)}, f32[8,128,1024]{2,1,0:T(8,128)}, u32[]{:S(2)}) %copy-start.3) | copy-done | bytes 4194328
  105.3 24.6 %shard_map.43 = (f32[8,128,1024]{2,1,0:T(8,128)S(1)}, f32[8,128,128]{2,1,0:T(8,128)S(1)}, f32[128,128]{1,0:T(8,128)S(1)}, f32[128,128]{1,0:T(8,128)S(1)}) custom-call(f32[8,128,1024]{2,1,0:T(8,128)S(1)} %copy-done.3, f32[8,128,128]{2,1,0:T(8,128)S(1)} %get-tuple-element.29.d_in, ...), custom_call_target="tpu_custom_call", output_to_operand_aliasing={{0}: (0, {}), {1}: (1, {}), {2}: (2, {}), {3}: (3, {})} | custom-call | flops 40000000000 | bytes 100000000 | tf_op jit(solution)/shard_map/pallas_call | solution.py:188
  130.0 0.0 copy-start.4
  130.0 2.0 %copy-done.4 = f32[8,128,1024]{2,1,0:T(8,128)} copy-done((f32[8,128,1024]{2,1,0:T(8,128)}, f32[8,128,1024]{2,1,0:T(8,128)S(1)}, u32[]{:S(2)}) %copy-start.4) | copy-done | bytes 4194328
  132.0 0.2 all-to-all-done.2.wq_ref
  132.2 1.6 %copy-done = f32[1024,512]{1,0:T(8,128)S(1)} copy-done((f32[1024,512]{1,0:T(8,128)S(1)}, f32[1024,512]{1,0:T(8,128)}, u32[]{:S(2)}) %copy-start) | copy-done | bytes 2097176
  133.8 2.2 %copy-done.5 = f32[8,128,1024]{2,1,0:T(8,128)S(1)} copy-done((f32[8,128,1024]{2,1,0:T(8,128)S(1)}, f32[8,128,1024]{2,1,0:T(8,128)}, u32[]{:S(2)}) %copy-start.5) | copy-done | bytes 4194328
  136.0 14.6 %shard_map.44 = (f32[1024,1024]{1,0:T(8,128)}, f32[1024,512]{1,0:T(8,128)}) custom-call(s32[2]{0:T(128)S(1)} %pad_add_fusion.at_ref, s32[2,128]{1,0:T(2,128)S(1)} %copy-done.1, f32[16,1024,128]{2,1,0:T(8,128)} %bitcast.7, f32[16,256,128]{2,1,0:T(8,128)S(1)} %all-to-all-done.2.wq_ref, f32[1024,512]{1,0:T(8,128)S(1)} %copy-done, ...), custom_call_target="tpu_custom_call" | custom-call | flops 10000000000 | bytes 20000000 | tf_op jit(solution)/shard_map/pallas_call | solution.py:309
  (7 shorter events, 0.0 us)
Async XLA Ops:
  8.9 26.8 %all-to-all-start = ((f32[16,64,128]{2,1,0:T(8,128)}), f32[16,64,128]{2,1,0:T(8,128)S(1)}, u32[]{:S(2)}, u32[]{:S(2)}) async-start(f32[16,64,128]{2,1,0:T(8,128)} %bitcast.3), calls=%async_computation | async-start | bytes 1048576 | tf_op jit(solution)/shard_map/all_to_all | solution.py:371
  20.4 111.8 %all-gather.3.cloned.1.call-start = ((), (), s32[]{:S(2)}) async-start(), calls=%async_computation.3 | async-start | bytes 8912896 | tf_op jit(solution)/shard_map/all_gather | solution.py:376
  36.6 28.0 %copy-start.6 = (f32[1024,128]{1,0:T(8,128)S(1)}, f32[1024,128]{1,0:T(8,128)}, u32[]{:S(2)}) copy-start(f32[1024,128]{1,0:T(8,128)} %slice.13) | copy-start | bytes 1572868
  59.7 13.2 %collective-permute-start.2 = (f32[16,3,64,128]{3,2,1,0:T(8,128)S(1)}, f32[16,3,64,128]{3,2,1,0:T(8,128)}, u32[]{:S(2)}, u32[]{:S(2)}) collective-permute-start(f32[16,3,64,128]{3,2,1,0:T(8,128)S(1)} %all_to_all.15.own_ref), channel_id=1, source_target_pairs={{0,1},{1,0},{2,3},{3,2},{4,5},{5,4},{6,7},{7,6},{8,9},{9,8},{10,11... | collective-permute-start | bytes 4718600 | tf_op jit(solution)/shard_map/ppermute | solution.py:380
  64.5 26.3 %collective-permute-start.1 = (f32[256,128]{1,0:T(8,128)S(1)}, f32[256,128]{1,0:T(8,128)S(1)}, u32[]{:S(2)}, u32[]{:S(2)}) collective-permute-start(f32[256,128]{1,0:T(8,128)S(1)} %get-tuple-element.34), channel_id=1, source_target_pairs={{0,16},{1,48},{2,80},{3,112},{4,144},{5,176},{6,208},{7,240},{16,1... | collective-permute-start | bytes 393224 | tf_op jit(solution)/shard_map/ppermute | solution.py:384
  66.6 24.3 %collective-permute-start = (f32[256,128]{1,0:T(8,128)S(1)}, f32[256,128]{1,0:T(8,128)S(1)}, u32[]{:S(2)}, u32[]{:S(2)}) collective-permute-start(f32[256,128]{1,0:T(8,128)S(1)} %get-tuple-element.35), channel_id=1, source_target_pairs={{0,0},{1,32},{2,64},{3,96},{4,128},{5,160},{6,192},{7,224},{16,17}... | collective-permute-start | bytes 393224 | tf_op jit(solution)/shard_map/ppermute | solution.py:384
  88.9 2.0 %copy-start.2 = (f32[8,128,1024]{2,1,0:T(8,128)}, f32[8,128,1024]{2,1,0:T(8,128)S(1)}, u32[]{:S(2)}) copy-start(f32[8,128,1024]{2,1,0:T(8,128)S(1)} %get-tuple-element.28.w_in) | copy-start | bytes 12582916
  92.4 39.8 %all-to-all-start.2 = ((f32[16,256,128]{2,1,0:T(8,128)}), f32[16,256,128]{2,1,0:T(8,128)S(1)}, u32[]{:S(2)}, u32[]{:S(2)}) async-start(f32[16,256,128]{2,1,0:T(8,128)} %broadcast_in_dim.10), calls=%async_computation.2 | async-start | bytes 4194304 | tf_op jit(solution)/shard_map/all_to_all | solution.py:395
  103.1 2.2 %copy-start.3 = (f32[8,128,1024]{2,1,0:T(8,128)S(1)}, f32[8,128,1024]{2,1,0:T(8,128)}, u32[]{:S(2)}) copy-start(f32[8,128,1024]{2,1,0:T(8,128)} %copy-done.2) | copy-start | bytes 12582916
  105.3 26.9 %copy-start.1 = (s32[2,128]{1,0:T(2,128)S(1)}, s32[2,128]{1,0:T(2,128)}, u32[]{:S(2)}) copy-start(s32[2,128]{1,0:T(2,128)} %pattern_ref.1) | copy-start | bytes 3076
  130.0 2.0 %copy-start.4 = (f32[8,128,1024]{2,1,0:T(8,128)}, f32[8,128,1024]{2,1,0:T(8,128)S(1)}, u32[]{:S(2)}) copy-start(f32[8,128,1024]{2,1,0:T(8,128)S(1)} %get-tuple-element.32.work) | copy-start | bytes 12582916
  132.2 1.6 %copy-start = (f32[1024,512]{1,0:T(8,128)S(1)}, f32[1024,512]{1,0:T(8,128)}, u32[]{:S(2)}) copy-start(f32[1024,512]{1,0:T(8,128)} %m_ref.1) | copy-start | bytes 6291460
  133.8 2.2 %copy-start.5 = (f32[8,128,1024]{2,1,0:T(8,128)S(1)}, f32[8,128,1024]{2,1,0:T(8,128)}, u32[]{:S(2)}) copy-start(f32[8,128,1024]{2,1,0:T(8,128)} %copy-done.4) | copy-start | bytes 12582916
Sparse Core Ops, SparseCore 0:
  35.8 70.0 all-gather.2

commit v6 on v5

--- a/solution.py
+++ b/solution.py
@@ -373,11 +373,11 @@
 
     place = jnp.stack([row, col]).astype(jnp.int32)
 
-    panel_cols = lax.all_gather(first, "col", axis=0)
-
     own = lax.all_to_all(pack(place, corner, rows), "row", 0, 0)
     first, own = lax.optimization_barrier((first, own))
     other = lax.ppermute(own, both, pairs(lambda r, c: (r, c ^ 1)))
+
+    panel_cols = lax.all_gather(first, "col", axis=0)
 
     span = matrix.shape[1] // 2
     shares = [

time: 158 us -> 157 us (level)
  no operation moved by 1% of the time
where the time goes in v6:
time: 157 us
  Pallas kernels  55.9 us (36%)
  starting transfers between devices  34.8 us (22%)
  blocking collectives  23.1 us (15%)
  local copies, waits for them, and re-layouts  15.2 us (10%)
  between operations  14.1 us (9%)
  waiting for transfers between devices  13.6 us (9%)
    pallas_call x2, Pallas kernels, factor_call(): pl.pallas_call(kernel, out_shape=STATE, in_specs=[pl.BlockSpec(memory_spa...  40.5 us
    all_to_all x1, blocking collectives, on_device(): own = lax.all_to_all(pack(place, corner, rows), 'row', 0, 0)  23.1 us
    pallas_call x1, Pallas kernels, tail(): pl.pallas_call(tail_kernel, grid_spec=grid_spec, out_shape=[jax.ShapeDtyp...  14.6 us
    all_to_all x1, waiting for transfers between devices, on_device(): corner = lax.all_to_all(corner, both, 0, 0, axis_index_groups=groups)  13.2 us
    all_to_all x1, starting transfers between devices, on_device(): corner = lax.all_to_all(corner, both, 0, 0, axis_index_groups=groups)  11.6 us
    unnamed x14, local copies, waits for them, and re-layouts  10.1 us
    all_to_all x1, starting transfers between devices, on_device(): lax.all_to_all(jnp.broadcast_to(share[None], (rows,) + share.shape), 'row...  9.82 us
    ppermute x2, starting transfers between devices, on_device(): lax.ppermute(first[h * span:(h + 1) * span], both, pairs(lambda r, c, h=h...  8.42 us
  transfers between devices with their start and end apart: 6, of which 2 were waited for; matrix products, arithmetic and copies ran while one was open for 2% of the time, Pallas kernels for 26%

profile of v6, /device:TPU:1, one launch (start us, length us, event | category | flops | bytes accessed | tf_op | source)
XLA Modules:
  0.0 156.8 jit_solution(6951997185535428218)
XLA Ops:
  7.2 0.8 slice.14
  8.0 0.8 broadcast_in_dim.4
  8.9 11.6 %all-to-all-start = ((f32[16,64,128]{2,1,0:T(8,128)}), f32[16,64,128]{2,1,0:T(8,128)S(1)}, u32[]{:S(2)}, u32[]{:S(2)}) async-start(f32[16,64,128]{2,1,0:T(8,128)} %bitcast.3), calls=%async_computation | async-start | bytes 1048576 | tf_op jit(solution)/shard_map/all_to_all | solution.py:371
  20.4 0.0 all-gather.3.cloned.1.call-start
  20.5 1.9 %slice.13 = f32[1024,128]{1,0:T(8,128)} slice(f32[1024,512]{1,0:T(8,128)} %m_ref.1), slice={[0:1024], [0:128]} | slice | bytes 1048576 | tf_op jit(solution)/shard_map/slice | solution.py:363
  22.4 0.1 pad_add_fusion.at_ref
  22.5 13.2 %all-to-all-done.corner_ref = f32[16,64,128]{2,1,0:T(8,128)S(1)} async-done(((f32[16,64,128]{2,1,0:T(8,128)}), f32[16,64,128]{2,1,0:T(8,128)S(1)}, u32[]{:S(2)}, u32[]{:S(2)}) %all-to-all-start) | async-done | bytes 524320 | tf_op jit(solution)/shard_map/all_to_all | solution.py:371
  35.7 0.8 shard_map.41
  36.5 0.0 copy-start.6
  36.5 23.1 %all_to_all.15.own_ref = f32[16,3,64,128]{3,2,1,0:T(8,128)S(1)} all-to-all(f32[16,3,64,128]{3,2,1,0:T(8,128)S(1)} %shard_map.41), channel_id=1, replica_groups=mesh['row'=16,'col'=16] {'row'}, dimensions={0} | all-to-all | bytes 3145728 | tf_op jit(solution)/shard_map/all_to_all | solution.py:376
  59.6 0.0 all-gather.3.cloned.1.call-update
  59.6 4.9 %collective-permute-start.2 = (f32[16,3,64,128]{3,2,1,0:T(8,128)S(1)}, f32[16,3,64,128]{3,2,1,0:T(8,128)}, u32[]{:S(2)}, u32[]{:S(2)}) collective-permute-start(f32[16,3,64,128]{3,2,1,0:T(8,128)S(1)} %all_to_all.15.own_ref), channel_id=1, source_target_pairs={{0,1},{1,0},{2,3},{3,2},{4,5},{5,4},{6,7},{7,6},{8,9},{9,8},{10,11... | collective-permute-start | bytes 4718600 | tf_op jit(solution)/shard_map/ppermute | solution.py:378
  64.5 0.0 copy-done.6
  64.6 2.1 %collective-permute-start.1 = (f32[256,128]{1,0:T(8,128)S(1)}, f32[256,128]{1,0:T(8,128)S(1)}, u32[]{:S(2)}, u32[]{:S(2)}) collective-permute-start(f32[256,128]{1,0:T(8,128)S(1)} %get-tuple-element.34), channel_id=1, source_target_pairs={{0,16},{1,48},{2,80},{3,112},{4,144},{5,176},{6,208},{7,240},{16,1... | collective-permute-start | bytes 393224 | tf_op jit(solution)/shard_map/ppermute | solution.py:384
  66.7 6.3 %collective-permute-start = (f32[256,128]{1,0:T(8,128)S(1)}, f32[256,128]{1,0:T(8,128)S(1)}, u32[]{:S(2)}, u32[]{:S(2)}) collective-permute-start(f32[256,128]{1,0:T(8,128)S(1)} %get-tuple-element.35), channel_id=1, source_target_pairs={{0,0},{1,32},{2,64},{3,96},{4,128},{5,160},{6,192},{7,224},{16,17}... | collective-permute-start | bytes 393224 | tf_op jit(solution)/shard_map/ppermute | solution.py:384
  73.0 0.0 collective-permute-done.2.other_ref
  73.0 15.9 %shard_map.42 = (f32[8,128,1024]{2,1,0:T(8,128)S(1)}, f32[8,128,128]{2,1,0:T(8,128)S(1)}, f32[128,128]{1,0:T(8,128)S(1)}, f32[128,128]{1,0:T(8,128)S(1)}) custom-call(s32[1]{0:T(128)} %bitcast.5.odd_ref, f32[16,3,64,128]{3,2,1,0:T(8,128)S(1)} %all_to_all.15.own_ref, f32[16,3,64,128]{3,2,1,0:T(8,128)} %collective-permute-done.2.other_ref), custom_call_target="tpu_custom_call" | custom-call | flops 30000001024 | bytes 75000000 | tf_op jit(solution)/shard_map/pallas_call | solution.py:188
  88.9 0.0 copy-start.2
  88.9 2.0 %copy-done.2 = f32[8,128,1024]{2,1,0:T(8,128)} copy-done((f32[8,128,1024]{2,1,0:T(8,128)}, f32[8,128,1024]{2,1,0:T(8,128)S(1)}, u32[]{:S(2)}) %copy-start.2) | copy-done | bytes 4194328
  90.9 0.0 collective-permute-done.1
  90.9 0.0 collective-permute-done
  91.0 1.5 broadcast_in_dim.10
  92.5 9.8 %all-to-all-start.2 = ((f32[16,256,128]{2,1,0:T(8,128)}), f32[16,256,128]{2,1,0:T(8,128)S(1)}, u32[]{:S(2)}, u32[]{:S(2)}) async-start(f32[16,256,128]{2,1,0:T(8,128)} %broadcast_in_dim.10), calls=%async_computation.2 | async-start | bytes 4194304 | tf_op jit(solution)/shard_map/all_to_all | solution.py:395
  102.3 0.0 copy-start.3
  102.3 2.3 %copy-done.3 = f32[8,128,1024]{2,1,0:T(8,128)S(1)} copy-done((f32[8,128,1024]{2,1,0:T(8,128)S(1)}, f32[8,128,1024]{2,1,0:T(8,128)}, u32[]{:S(2)}) %copy-start.3) | copy-done | bytes 4194328
  104.6 24.6 %shard_map.43 = (f32[8,128,1024]{2,1,0:T(8,128)S(1)}, f32[8,128,128]{2,1,0:T(8,128)S(1)}, f32[128,128]{1,0:T(8,128)S(1)}, f32[128,128]{1,0:T(8,128)S(1)}) custom-call(f32[8,128,1024]{2,1,0:T(8,128)S(1)} %copy-done.3, f32[8,128,128]{2,1,0:T(8,128)S(1)} %get-tuple-element.29.d_in, ...), custom_call_target="tpu_custom_call", output_to_operand_aliasing={{0}: (0, {}), {1}: (1, {}), {2}: (2, {}), {3}: (3, {})} | custom-call | flops 40000000000 | bytes 100000000 | tf_op jit(solution)/shard_map/pallas_call | solution.py:188
  129.2 0.0 copy-start.4
  129.2 2.0 %copy-done.4 = f32[8,128,1024]{2,1,0:T(8,128)} copy-done((f32[8,128,1024]{2,1,0:T(8,128)}, f32[8,128,1024]{2,1,0:T(8,128)S(1)}, u32[]{:S(2)}) %copy-start.4) | copy-done | bytes 4194328
  131.3 0.3 all-to-all-done.2.wq_ref
  131.6 1.6 %copy-done = f32[1024,512]{1,0:T(8,128)S(1)} copy-done((f32[1024,512]{1,0:T(8,128)S(1)}, f32[1024,512]{1,0:T(8,128)}, u32[]{:S(2)}) %copy-start) | copy-done | bytes 2097176
  133.1 2.2 %copy-done.5 = f32[8,128,1024]{2,1,0:T(8,128)S(1)} copy-done((f32[8,128,1024]{2,1,0:T(8,128)S(1)}, f32[8,128,1024]{2,1,0:T(8,128)}, u32[]{:S(2)}) %copy-start.5) | copy-done | bytes 4194328
  135.3 14.6 %shard_map.44 = (f32[1024,1024]{1,0:T(8,128)}, f32[1024,512]{1,0:T(8,128)}) custom-call(s32[2]{0:T(128)S(1)} %pad_add_fusion.at_ref, s32[2,128]{1,0:T(2,128)S(1)} %copy-done.1, f32[16,1024,128]{2,1,0:T(8,128)} %bitcast.7, f32[16,256,128]{2,1,0:T(8,128)S(1)} %all-to-all-done.2.wq_ref, f32[1024,512]{1,0:T(8,128)S(1)} %copy-done, ...), custom_call_target="tpu_custom_call" | custom-call | flops 10000000000 | bytes 20000000 | tf_op jit(solution)/shard_map/pallas_call | solution.py:309
  (7 shorter events, 0.0 us)
Async XLA Ops:
  8.9 26.8 %all-to-all-start = ((f32[16,64,128]{2,1,0:T(8,128)}), f32[16,64,128]{2,1,0:T(8,128)S(1)}, u32[]{:S(2)}, u32[]{:S(2)}) async-start(f32[16,64,128]{2,1,0:T(8,128)} %bitcast.3), calls=%async_computation | async-start | bytes 1048576 | tf_op jit(solution)/shard_map/all_to_all | solution.py:371
  20.4 111.1 %all-gather.3.cloned.1.call-start = ((), (), s32[]{:S(2)}) async-start(), calls=%async_computation.3 | async-start | bytes 8912896 | tf_op jit(solution)/shard_map/all_gather | solution.py:380
  36.5 28.1 %copy-start.6 = (f32[1024,128]{1,0:T(8,128)S(1)}, f32[1024,128]{1,0:T(8,128)}, u32[]{:S(2)}) copy-start(f32[1024,128]{1,0:T(8,128)} %slice.13) | copy-start | bytes 1572868
  59.6 13.4 %collective-permute-start.2 = (f32[16,3,64,128]{3,2,1,0:T(8,128)S(1)}, f32[16,3,64,128]{3,2,1,0:T(8,128)}, u32[]{:S(2)}, u32[]{:S(2)}) collective-permute-start(f32[16,3,64,128]{3,2,1,0:T(8,128)S(1)} %all_to_all.15.own_ref), channel_id=1, source_target_pairs={{0,1},{1,0},{2,3},{3,2},{4,5},{5,4},{6,7},{7,6},{8,9},{9,8},{10,11... | collective-permute-start | bytes 4718600 | tf_op jit(solution)/shard_map/ppermute | solution.py:378
  64.6 26.4 %collective-permute-start.1 = (f32[256,128]{1,0:T(8,128)S(1)}, f32[256,128]{1,0:T(8,128)S(1)}, u32[]{:S(2)}, u32[]{:S(2)}) collective-permute-start(f32[256,128]{1,0:T(8,128)S(1)} %get-tuple-element.34), channel_id=1, source_target_pairs={{0,16},{1,48},{2,80},{3,112},{4,144},{5,176},{6,208},{7,240},{16,1... | collective-permute-start | bytes 393224 | tf_op jit(solution)/shard_map/ppermute | solution.py:384
  66.7 24.3 %collective-permute-start = (f32[256,128]{1,0:T(8,128)S(1)}, f32[256,128]{1,0:T(8,128)S(1)}, u32[]{:S(2)}, u32[]{:S(2)}) collective-permute-start(f32[256,128]{1,0:T(8,128)S(1)} %get-tuple-element.35), channel_id=1, source_target_pairs={{0,0},{1,32},{2,64},{3,96},{4,128},{5,160},{6,192},{7,224},{16,17}... | collective-permute-start | bytes 393224 | tf_op jit(solution)/shard_map/ppermute | solution.py:384
  88.9 2.0 %copy-start.2 = (f32[8,128,1024]{2,1,0:T(8,128)}, f32[8,128,1024]{2,1,0:T(8,128)S(1)}, u32[]{:S(2)}) copy-start(f32[8,128,1024]{2,1,0:T(8,128)S(1)} %get-tuple-element.28.w_in) | copy-start | bytes 12582916
  92.5 39.1 %all-to-all-start.2 = ((f32[16,256,128]{2,1,0:T(8,128)}), f32[16,256,128]{2,1,0:T(8,128)S(1)}, u32[]{:S(2)}, u32[]{:S(2)}) async-start(f32[16,256,128]{2,1,0:T(8,128)} %broadcast_in_dim.10), calls=%async_computation.2 | async-start | bytes 4194304 | tf_op jit(solution)/shard_map/all_to_all | solution.py:395
  102.3 2.3 %copy-start.3 = (f32[8,128,1024]{2,1,0:T(8,128)S(1)}, f32[8,128,1024]{2,1,0:T(8,128)}, u32[]{:S(2)}) copy-start(f32[8,128,1024]{2,1,0:T(8,128)} %copy-done.2) | copy-start | bytes 12582916
  104.6 27.0 %copy-start.1 = (s32[2,128]{1,0:T(2,128)S(1)}, s32[2,128]{1,0:T(2,128)}, u32[]{:S(2)}) copy-start(s32[2,128]{1,0:T(2,128)} %pattern_ref.1) | copy-start | bytes 3076
  129.2 2.0 %copy-start.4 = (f32[8,128,1024]{2,1,0:T(8,128)}, f32[8,128,1024]{2,1,0:T(8,128)S(1)}, u32[]{:S(2)}) copy-start(f32[8,128,1024]{2,1,0:T(8,128)S(1)} %get-tuple-element.32.work) | copy-start | bytes 12582916
  131.6 1.6 %copy-start = (f32[1024,512]{1,0:T(8,128)S(1)}, f32[1024,512]{1,0:T(8,128)}, u32[]{:S(2)}) copy-start(f32[1024,512]{1,0:T(8,128)} %m_ref.1) | copy-start | bytes 6291460
  133.1 2.2 %copy-start.5 = (f32[8,128,1024]{2,1,0:T(8,128)S(1)}, f32[8,128,1024]{2,1,0:T(8,128)}, u32[]{:S(2)}) copy-start(f32[8,128,1024]{2,1,0:T(8,128)} %copy-done.4) | copy-start | bytes 12582916
Sparse Core Ops, SparseCore 0:
  59.8 68.6 all-gather.2

commit v7 on v6

--- a/solution.py
+++ b/solution.py
@@ -145,7 +145,7 @@
     lax.fori_loop(first, last, step, 0)
 
 
-FIRST_STEPS = 2
+FIRST_STEPS = 3
 
 
 def start_kernel(odd_ref, own_ref, other_ref, work, diag, head, base):
@@ -360,6 +360,8 @@
     def pairs(target, width=cols):
         return [(at(r, c), at(*target(r, c))) for r in range(rows) for c in range(width)]
 
+    panel_cols = lax.all_gather(matrix[:, :BLK], "col", axis=0)
+
     first = matrix[:, :BLK]
     cut = BLK // 2
     groups = [
@@ -376,8 +378,6 @@
     own = lax.all_to_all(pack(place, corner, rows), "row", 0, 0)
     first, own = lax.optimization_barrier((first, own))
     other = lax.ppermute(own, both, pairs(lambda r, c: (r, c ^ 1)))
-
-    panel_cols = lax.all_gather(first, "col", axis=0)
 
     span = matrix.shape[1] // 2
     shares = [

time: 157 us -> 164 us (1.045); the launches traced: 157 us -> 161 us
  waiting for transfers between devices: 13.6 us -> 24.1 us
  starting transfers between devices: 34.8 us -> 31.5 us
  blocking collectives: 23.1 us -> 20.4 us
    all_to_all x1, waiting for transfers between devices: 13.2 us -> 18.9 us  [on_device(): corner = lax.all_to_all(corner, both, 0, 0, axis_index_groups=groups)]
    all_to_all x1, waiting for transfers between devices: 0.29 us -> 5.15 us  [on_device(): lax.all_to_all(jnp.broadcast_to(share[None], (rows,) + share.shape), 'row...]
    all_to_all x1, starting transfers between devices: 9.82 us -> 6.45 us  [on_device(): lax.all_to_all(jnp.broadcast_to(share[None], (rows,) + share.shape), 'row...]
    all_to_all x1, blocking collectives: 23.1 us -> 20.4 us  [on_device(): own = lax.all_to_all(pack(place, corner, rows), 'row', 0, 0)]
    ppermute x1, starting transfers between devices: 4.89 us -> 7.53 us  [on_device(): other = lax.ppermute(own, both, pairs(lambda r, c: (r, c ^ 1)))]
    ppermute x2, starting transfers between devices: 8.42 us -> 5.94 us  [on_device(): lax.ppermute(first[h * span:(h + 1) * span], both, pairs(lambda r, c, h=h...]
where the time goes in v7:
time: 164 us; the launch traced here: 161 us
  Pallas kernels  56 us (34%)
  starting transfers between devices  31.5 us (19%)
  waiting for transfers between devices  24.1 us (15%)
  blocking collectives  20.4 us (12%)
  local copies, waits for them, and re-layouts  15.1 us (9%)
  between operations  14.1 us (9%)
    pallas_call x2, Pallas kernels, factor_call(): pl.pallas_call(kernel, out_shape=STATE, in_specs=[pl.BlockSpec(memory_spa...  40.7 us
    all_to_all x1, blocking collectives, on_device(): own = lax.all_to_all(pack(place, corner, rows), 'row', 0, 0)  20.4 us
    all_to_all x1, waiting for transfers between devices, on_device(): corner = lax.all_to_all(corner, both, 0, 0, axis_index_groups=groups)  18.9 us
    pallas_call x1, Pallas kernels, tail(): pl.pallas_call(tail_kernel, grid_spec=grid_spec, out_shape=[jax.ShapeDtyp...  14.6 us
    all_to_all x1, starting transfers between devices, on_device(): corner = lax.all_to_all(corner, both, 0, 0, axis_index_groups=groups)  11.6 us
    unnamed x14, local copies, waits for them, and re-layouts  9.99 us
    ppermute x1, starting transfers between devices, on_device(): other = lax.ppermute(own, both, pairs(lambda r, c: (r, c ^ 1)))  7.53 us
    all_to_all x1, starting transfers between devices, on_device(): lax.all_to_all(jnp.broadcast_to(share[None], (rows,) + share.shape), 'row...  6.45 us
  transfers between devices with their start and end apart: 6, of which 2 were waited for; matrix products, arithmetic and copies ran while one was open for 2% of the time, Pallas kernels for 26%

profile of v7, /device:TPU:1, one launch (start us, length us, event | category | flops | bytes accessed | tf_op | source)
XLA Modules:
  0.0 161.3 jit_solution(178731467119297275)
XLA Ops:
  7.2 0.0 all-gather.3.cloned.1.call-start
  7.2 1.9 %slice.14 = f32[1024,128]{1,0:T(8,128)} slice(f32[1024,512]{1,0:T(8,128)} %m_ref.1), slice={[0:1024], [0:128]} | slice | bytes 1048576 | tf_op jit(solution)/shard_map/slice | solution.py:363
  9.1 0.0 all-gather.3.cloned.1.call-update
  9.1 0.8 slice.15
  10.0 0.8 broadcast_in_dim.4
  10.8 11.6 %all-to-all-start = ((f32[16,64,128]{2,1,0:T(8,128)}), f32[16,64,128]{2,1,0:T(8,128)S(1)}, u32[]{:S(2)}, u32[]{:S(2)}) async-start(f32[16,64,128]{2,1,0:T(8,128)} %bitcast.4), calls=%async_computation | async-start | bytes 1048576 | tf_op jit(solution)/shard_map/all_to_all | solution.py:373
  22.4 0.1 pad_add_fusion.at_ref
  22.5 18.9 %all-to-all-done.corner_ref = f32[16,64,128]{2,1,0:T(8,128)S(1)} async-done(((f32[16,64,128]{2,1,0:T(8,128)}), f32[16,64,128]{2,1,0:T(8,128)S(1)}, u32[]{:S(2)}, u32[]{:S(2)}) %all-to-all-start) | async-done | bytes 524320 | tf_op jit(solution)/shard_map/all_to_all | solution.py:373
  41.4 0.8 shard_map.41
  42.2 0.0 copy-start.6
  42.2 20.4 %all_to_all.15.own_ref = f32[16,3,64,128]{3,2,1,0:T(8,128)S(1)} all-to-all(f32[16,3,64,128]{3,2,1,0:T(8,128)S(1)} %shard_map.41), channel_id=1, replica_groups=mesh['row'=16,'col'=16] {'row'}, dimensions={0} | all-to-all | bytes 3145728 | tf_op jit(solution)/shard_map/all_to_all | solution.py:378
  62.5 7.5 %collective-permute-start.2 = (f32[16,3,64,128]{3,2,1,0:T(8,128)S(1)}, f32[16,3,64,128]{3,2,1,0:T(8,128)}, u32[]{:S(2)}, u32[]{:S(2)}) collective-permute-start(f32[16,3,64,128]{3,2,1,0:T(8,128)S(1)} %all_to_all.15.own_ref), channel_id=1, source_target_pairs={{0,1},{1,0},{2,3},{3,2},{4,5},{5,4},{6,7},{7,6},{8,9},{9,8},{10,11... | collective-permute-start | bytes 4718600 | tf_op jit(solution)/shard_map/ppermute | solution.py:380
  70.1 0.0 copy-done.6
  70.1 2.1 %collective-permute-start.1 = (f32[256,128]{1,0:T(8,128)S(1)}, f32[256,128]{1,0:T(8,128)S(1)}, u32[]{:S(2)}, u32[]{:S(2)}) collective-permute-start(f32[256,128]{1,0:T(8,128)S(1)} %get-tuple-element.34), channel_id=1, source_target_pairs={{0,16},{1,48},{2,80},{3,112},{4,144},{5,176},{6,208},{7,240},{16,1... | collective-permute-start | bytes 393224 | tf_op jit(solution)/shard_map/ppermute | solution.py:384
  72.2 3.9 %collective-permute-start = (f32[256,128]{1,0:T(8,128)S(1)}, f32[256,128]{1,0:T(8,128)S(1)}, u32[]{:S(2)}, u32[]{:S(2)}) collective-permute-start(f32[256,128]{1,0:T(8,128)S(1)} %get-tuple-element.35), channel_id=1, source_target_pairs={{0,0},{1,32},{2,64},{3,96},{4,128},{5,160},{6,192},{7,224},{16,17}... | collective-permute-start | bytes 393224 | tf_op jit(solution)/shard_map/ppermute | solution.py:384
  76.0 0.0 collective-permute-done.2.other_ref
  76.1 20.9 %shard_map.42 = (f32[8,128,1024]{2,1,0:T(8,128)S(1)}, f32[8,128,128]{2,1,0:T(8,128)S(1)}, f32[128,128]{1,0:T(8,128)S(1)}, f32[128,128]{1,0:T(8,128)S(1)}) custom-call(s32[1]{0:T(128)} %bitcast.5.odd_ref, f32[16,3,64,128]{3,2,1,0:T(8,128)S(1)} %all_to_all.15.own_ref, f32[16,3,64,128]{3,2,1,0:T(8,128)} %collective-permute-done.2.other_ref), custom_call_target="tpu_custom_call" | custom-call | flops 30000001024 | bytes 75000000 | tf_op jit(solution)/shard_map/pallas_call | solution.py:188
  97.0 0.0 copy-start.2
  97.0 2.0 %copy-done.2 = f32[8,128,1024]{2,1,0:T(8,128)} copy-done((f32[8,128,1024]{2,1,0:T(8,128)}, f32[8,128,1024]{2,1,0:T(8,128)S(1)}, u32[]{:S(2)}) %copy-start.2) | copy-done | bytes 4194328
  99.0 0.0 collective-permute-done.1
  99.0 0.0 collective-permute-done
  99.0 1.5 broadcast_in_dim.10
  100.5 6.4 %all-to-all-start.2 = ((f32[16,256,128]{2,1,0:T(8,128)}), f32[16,256,128]{2,1,0:T(8,128)S(1)}, u32[]{:S(2)}, u32[]{:S(2)}) async-start(f32[16,256,128]{2,1,0:T(8,128)} %broadcast_in_dim.10), calls=%async_computation.2 | async-start | bytes 4194304 | tf_op jit(solution)/shard_map/all_to_all | solution.py:395
  107.0 0.0 copy-start.3
  107.0 2.2 %copy-done.3 = f32[8,128,1024]{2,1,0:T(8,128)S(1)} copy-done((f32[8,128,1024]{2,1,0:T(8,128)S(1)}, f32[8,128,1024]{2,1,0:T(8,128)}, u32[]{:S(2)}) %copy-start.3) | copy-done | bytes 4194328
  109.2 19.8 %shard_map.43 = (f32[8,128,1024]{2,1,0:T(8,128)S(1)}, f32[8,128,128]{2,1,0:T(8,128)S(1)}, f32[128,128]{1,0:T(8,128)S(1)}, f32[128,128]{1,0:T(8,128)S(1)}) custom-call(f32[8,128,1024]{2,1,0:T(8,128)S(1)} %copy-done.3, f32[8,128,128]{2,1,0:T(8,128)S(1)} %get-tuple-element.29.d_in, ...), custom_call_target="tpu_custom_call", output_to_operand_aliasing={{0}: (0, {}), {1}: (1, {}), {2}: (2, {}), {3}: (3, {})} | custom-call | flops 40000000000 | bytes 100000000 | tf_op jit(solution)/shard_map/pallas_call | solution.py:188
  128.9 0.0 copy-start.4
  129.0 2.0 %copy-done.4 = f32[8,128,1024]{2,1,0:T(8,128)} copy-done((f32[8,128,1024]{2,1,0:T(8,128)}, f32[8,128,1024]{2,1,0:T(8,128)S(1)}, u32[]{:S(2)}) %copy-start.4) | copy-done | bytes 4194328
  131.0 5.2 %all-to-all-done.2.wq_ref = f32[16,256,128]{2,1,0:T(8,128)S(1)} async-done(((f32[16,256,128]{2,1,0:T(8,128)}), f32[16,256,128]{2,1,0:T(8,128)S(1)}, u32[]{:S(2)}, u32[]{:S(2)}) %all-to-all-start.2) | async-done | bytes 2097184 | tf_op jit(solution)/shard_map/all_to_all | solution.py:395
  136.1 1.6 copy-done
  137.7 2.2 %copy-done.5 = f32[8,128,1024]{2,1,0:T(8,128)S(1)} copy-done((f32[8,128,1024]{2,1,0:T(8,128)S(1)}, f32[8,128,1024]{2,1,0:T(8,128)}, u32[]{:S(2)}) %copy-start.5) | copy-done | bytes 4194328
  139.9 14.6 %shard_map.44 = (f32[1024,1024]{1,0:T(8,128)}, f32[1024,512]{1,0:T(8,128)}) custom-call(s32[2]{0:T(128)S(1)} %pad_add_fusion.at_ref, s32[2,128]{1,0:T(2,128)S(1)} %copy-done.1, f32[16,1024,128]{2,1,0:T(8,128)} %bitcast.7, f32[16,256,128]{2,1,0:T(8,128)S(1)} %all-to-all-done.2.wq_ref, f32[1024,512]{1,0:T(8,128)S(1)} %copy-done, ...), custom_call_target="tpu_custom_call" | custom-call | flops 10000000000 | bytes 20000000 | tf_op jit(solution)/shard_map/pallas_call | solution.py:309
  (7 shorter events, 0.0 us)
Async XLA Ops:
  7.2 128.9 %all-gather.3.cloned.1.call-start = ((), (), s32[]{:S(2)}) async-start(), calls=%async_computation.3 | async-start | bytes 8912896 | tf_op jit(solution)/shard_map/all_gather | solution.py:363
  10.8 30.6 %all-to-all-start = ((f32[16,64,128]{2,1,0:T(8,128)}), f32[16,64,128]{2,1,0:T(8,128)S(1)}, u32[]{:S(2)}, u32[]{:S(2)}) async-start(f32[16,64,128]{2,1,0:T(8,128)} %bitcast.4), calls=%async_computation | async-start | bytes 1048576 | tf_op jit(solution)/shard_map/all_to_all | solution.py:373
  42.2 27.9 %copy-start.6 = (f32[1024,128]{1,0:T(8,128)S(1)}, f32[1024,128]{1,0:T(8,128)}, u32[]{:S(2)}) copy-start(f32[1024,128]{1,0:T(8,128)} %slice.14) | copy-start | bytes 1572868
  62.5 13.5 %collective-permute-start.2 = (f32[16,3,64,128]{3,2,1,0:T(8,128)S(1)}, f32[16,3,64,128]{3,2,1,0:T(8,128)}, u32[]{:S(2)}, u32[]{:S(2)}) collective-permute-start(f32[16,3,64,128]{3,2,1,0:T(8,128)S(1)} %all_to_all.15.own_ref), channel_id=1, source_target_pairs={{0,1},{1,0},{2,3},{3,2},{4,5},{5,4},{6,7},{7,6},{8,9},{9,8},{10,11... | collective-permute-start | bytes 4718600 | tf_op jit(solution)/shard_map/ppermute | solution.py:380
  70.1 28.9 %collective-permute-start.1 = (f32[256,128]{1,0:T(8,128)S(1)}, f32[256,128]{1,0:T(8,128)S(1)}, u32[]{:S(2)}, u32[]{:S(2)}) collective-permute-start(f32[256,128]{1,0:T(8,128)S(1)} %get-tuple-element.34), channel_id=1, source_target_pairs={{0,16},{1,48},{2,80},{3,112},{4,144},{5,176},{6,208},{7,240},{16,1... | collective-permute-start | bytes 393224 | tf_op jit(solution)/shard_map/ppermute | solution.py:384
  72.2 26.8 %collective-permute-start = (f32[256,128]{1,0:T(8,128)S(1)}, f32[256,128]{1,0:T(8,128)S(1)}, u32[]{:S(2)}, u32[]{:S(2)}) collective-permute-start(f32[256,128]{1,0:T(8,128)S(1)} %get-tuple-element.35), channel_id=1, source_target_pairs={{0,0},{1,32},{2,64},{3,96},{4,128},{5,160},{6,192},{7,224},{16,17}... | collective-permute-start | bytes 393224 | tf_op jit(solution)/shard_map/ppermute | solution.py:384
  97.0 2.0 %copy-start.2 = (f32[8,128,1024]{2,1,0:T(8,128)}, f32[8,128,1024]{2,1,0:T(8,128)S(1)}, u32[]{:S(2)}) copy-start(f32[8,128,1024]{2,1,0:T(8,128)S(1)} %get-tuple-element.28.w_in) | copy-start | bytes 12582916
  100.5 35.6 %all-to-all-start.2 = ((f32[16,256,128]{2,1,0:T(8,128)}), f32[16,256,128]{2,1,0:T(8,128)S(1)}, u32[]{:S(2)}, u32[]{:S(2)}) async-start(f32[16,256,128]{2,1,0:T(8,128)} %broadcast_in_dim.10), calls=%async_computation.2 | async-start | bytes 4194304 | tf_op jit(solution)/shard_map/all_to_all | solution.py:395
  107.0 2.2 %copy-start.3 = (f32[8,128,1024]{2,1,0:T(8,128)S(1)}, f32[8,128,1024]{2,1,0:T(8,128)}, u32[]{:S(2)}) copy-start(f32[8,128,1024]{2,1,0:T(8,128)} %copy-done.2) | copy-start | bytes 12582916
  109.2 26.9 %copy-start.1 = (s32[2,128]{1,0:T(2,128)S(1)}, s32[2,128]{1,0:T(2,128)}, u32[]{:S(2)}) copy-start(s32[2,128]{1,0:T(2,128)} %pattern_ref.1) | copy-start | bytes 3076
  128.9 2.0 %copy-start.4 = (f32[8,128,1024]{2,1,0:T(8,128)}, f32[8,128,1024]{2,1,0:T(8,128)S(1)}, u32[]{:S(2)}) copy-start(f32[8,128,1024]{2,1,0:T(8,128)S(1)} %get-tuple-element.32.work) | copy-start | bytes 12582916
  136.1 1.6 copy-start
  137.7 2.2 %copy-start.5 = (f32[8,128,1024]{2,1,0:T(8,128)S(1)}, f32[8,128,1024]{2,1,0:T(8,128)}, u32[]{:S(2)}) copy-start(f32[8,128,1024]{2,1,0:T(8,128)} %copy-done.4) | copy-start | bytes 12582916
Sparse Core Ops, SparseCore 0:
  9.8 80.4 all-gather.2

commit v8 on v5

--- a/solution.py
+++ b/solution.py
@@ -204,7 +204,7 @@
     )
 
 
-TILE = 512
+TILE = 256
 STEP = 256
 
 

time: 158 us -> 158 us (level)
  no operation moved by 1% of the time
where the time goes in v8:
time: 158 us
  Pallas kernels  56.2 us (36%)
  starting transfers between devices  35.4 us (22%)
  blocking collectives  23.1 us (15%)
  local copies, waits for them, and re-layouts  15.1 us (10%)
  between operations  14.1 us (9%)
  waiting for transfers between devices  13.6 us (9%)
    pallas_call x2, Pallas kernels, factor_call(): pl.pallas_call(kernel, out_shape=STATE, in_specs=[pl.BlockSpec(memory_spa...  40.6 us
    all_to_all x1, blocking collectives, on_device(): own = lax.all_to_all(pack(place, corner, rows), 'row', 0, 0)  23.1 us
    pallas_call x1, Pallas kernels, tail(): pl.pallas_call(tail_kernel, grid_spec=grid_spec, out_shape=[jax.ShapeDtyp...  14.9 us
    all_to_all x1, waiting for transfers between devices, on_device(): corner = lax.all_to_all(corner, both, 0, 0, axis_index_groups=groups)  13.3 us
    all_to_all x1, starting transfers between devices, on_device(): corner = lax.all_to_all(corner, both, 0, 0, axis_index_groups=groups)  11.6 us
    all_to_all x1, starting transfers between devices, on_device(): lax.all_to_all(jnp.broadcast_to(share[None], (rows,) + share.shape), 'row...  10.7 us
    unnamed x14, local copies, waits for them, and re-layouts  10 us
    ppermute x2, starting transfers between devices, on_device(): lax.ppermute(first[h * span:(h + 1) * span], both, pairs(lambda r, c, h=h...  8.37 us
  transfers between devices with their start and end apart: 6, of which 2 were waited for; matrix products, arithmetic and copies ran while one was open for 2% of the time, Pallas kernels for 26%

profile of v8, /device:TPU:1, one launch (start us, length us, event | category | flops | bytes accessed | tf_op | source)
XLA Modules:
  0.0 157.8 jit_solution(2820656480317691880)
XLA Ops:
  7.2 0.8 slice.14
  8.0 0.8 broadcast_in_dim.4
  8.9 11.6 %all-to-all-start = ((f32[16,64,128]{2,1,0:T(8,128)}), f32[16,64,128]{2,1,0:T(8,128)S(1)}, u32[]{:S(2)}, u32[]{:S(2)}) async-start(f32[16,64,128]{2,1,0:T(8,128)} %bitcast.3), calls=%async_computation | async-start | bytes 1048576 | tf_op jit(solution)/shard_map/all_to_all | solution.py:371
  20.4 0.0 all-gather.3.cloned.1.call-start
  20.5 1.9 %slice.13 = f32[1024,128]{1,0:T(8,128)} slice(f32[1024,512]{1,0:T(8,128)} %m_ref.1), slice={[0:1024], [0:128]} | slice | bytes 1048576 | tf_op jit(solution)/shard_map/slice | solution.py:363
  22.4 13.3 %all-to-all-done.corner_ref = f32[16,64,128]{2,1,0:T(8,128)S(1)} async-done(((f32[16,64,128]{2,1,0:T(8,128)}), f32[16,64,128]{2,1,0:T(8,128)S(1)}, u32[]{:S(2)}, u32[]{:S(2)}) %all-to-all-start) | async-done | bytes 524320 | tf_op jit(solution)/shard_map/all_to_all | solution.py:371
  35.7 0.0 all-gather.3.cloned.1.call-update
  35.7 0.1 pad_add_fusion.at_ref
  35.8 0.8 shard_map.41
  36.6 0.0 copy-start.6
  36.6 23.1 %all_to_all.15.own_ref = f32[16,3,64,128]{3,2,1,0:T(8,128)S(1)} all-to-all(f32[16,3,64,128]{3,2,1,0:T(8,128)S(1)} %shard_map.41), channel_id=1, replica_groups=mesh['row'=16,'col'=16] {'row'}, dimensions={0} | all-to-all | bytes 3145728 | tf_op jit(solution)/shard_map/all_to_all | solution.py:378
  59.7 4.8 %collective-permute-start.2 = (f32[16,3,64,128]{3,2,1,0:T(8,128)S(1)}, f32[16,3,64,128]{3,2,1,0:T(8,128)}, u32[]{:S(2)}, u32[]{:S(2)}) collective-permute-start(f32[16,3,64,128]{3,2,1,0:T(8,128)S(1)} %all_to_all.15.own_ref), channel_id=1, source_target_pairs={{0,1},{1,0},{2,3},{3,2},{4,5},{5,4},{6,7},{7,6},{8,9},{9,8},{10,11... | collective-permute-start | bytes 4718600 | tf_op jit(solution)/shard_map/ppermute | solution.py:380
  64.5 0.0 copy-done.6
  64.5 2.1 %collective-permute-start.1 = (f32[256,128]{1,0:T(8,128)S(1)}, f32[256,128]{1,0:T(8,128)S(1)}, u32[]{:S(2)}, u32[]{:S(2)}) collective-permute-start(f32[256,128]{1,0:T(8,128)S(1)} %get-tuple-element.34), channel_id=1, source_target_pairs={{0,16},{1,48},{2,80},{3,112},{4,144},{5,176},{6,208},{7,240},{16,1... | collective-permute-start | bytes 393224 | tf_op jit(solution)/shard_map/ppermute | solution.py:384
  66.6 6.3 %collective-permute-start = (f32[256,128]{1,0:T(8,128)S(1)}, f32[256,128]{1,0:T(8,128)S(1)}, u32[]{:S(2)}, u32[]{:S(2)}) collective-permute-start(f32[256,128]{1,0:T(8,128)S(1)} %get-tuple-element.35), channel_id=1, source_target_pairs={{0,0},{1,32},{2,64},{3,96},{4,128},{5,160},{6,192},{7,224},{16,17}... | collective-permute-start | bytes 393224 | tf_op jit(solution)/shard_map/ppermute | solution.py:384
  72.9 0.0 collective-permute-done.2.other_ref
  72.9 15.9 %shard_map.42 = (f32[8,128,1024]{2,1,0:T(8,128)S(1)}, f32[8,128,128]{2,1,0:T(8,128)S(1)}, f32[128,128]{1,0:T(8,128)S(1)}, f32[128,128]{1,0:T(8,128)S(1)}) custom-call(s32[1]{0:T(128)} %bitcast.5.odd_ref, f32[16,3,64,128]{3,2,1,0:T(8,128)S(1)} %all_to_all.15.own_ref, f32[16,3,64,128]{3,2,1,0:T(8,128)} %collective-permute-done.2.other_ref), custom_call_target="tpu_custom_call" | custom-call | flops 30000001024 | bytes 75000000 | tf_op jit(solution)/shard_map/pallas_call | solution.py:188
  88.9 0.0 copy-start.2
  88.9 2.0 %copy-done.2 = f32[8,128,1024]{2,1,0:T(8,128)} copy-done((f32[8,128,1024]{2,1,0:T(8,128)}, f32[8,128,1024]{2,1,0:T(8,128)S(1)}, u32[]{:S(2)}) %copy-start.2) | copy-done | bytes 4194328
  90.9 0.0 collective-permute-done.1
  90.9 0.0 collective-permute-done
  90.9 1.5 broadcast_in_dim.10
  92.4 10.7 %all-to-all-start.2 = ((f32[16,256,128]{2,1,0:T(8,128)}), f32[16,256,128]{2,1,0:T(8,128)S(1)}, u32[]{:S(2)}, u32[]{:S(2)}) async-start(f32[16,256,128]{2,1,0:T(8,128)} %broadcast_in_dim.10), calls=%async_computation.2 | async-start | bytes 4194304 | tf_op jit(solution)/shard_map/all_to_all | solution.py:395
  103.1 0.0 copy-start.3
  103.1 2.2 %copy-done.3 = f32[8,128,1024]{2,1,0:T(8,128)S(1)} copy-done((f32[8,128,1024]{2,1,0:T(8,128)S(1)}, f32[8,128,1024]{2,1,0:T(8,128)}, u32[]{:S(2)}) %copy-start.3) | copy-done | bytes 4194328
  105.3 24.6 %shard_map.43 = (f32[8,128,1024]{2,1,0:T(8,128)S(1)}, f32[8,128,128]{2,1,0:T(8,128)S(1)}, f32[128,128]{1,0:T(8,128)S(1)}, f32[128,128]{1,0:T(8,128)S(1)}) custom-call(f32[8,128,1024]{2,1,0:T(8,128)S(1)} %copy-done.3, f32[8,128,128]{2,1,0:T(8,128)S(1)} %get-tuple-element.29.d_in, ...), custom_call_target="tpu_custom_call", output_to_operand_aliasing={{0}: (0, {}), {1}: (1, {}), {2}: (2, {}), {3}: (3, {})} | custom-call | flops 40000000000 | bytes 100000000 | tf_op jit(solution)/shard_map/pallas_call | solution.py:188
  130.0 0.0 copy-start.4
  130.0 2.0 %copy-done.4 = f32[8,128,1024]{2,1,0:T(8,128)} copy-done((f32[8,128,1024]{2,1,0:T(8,128)}, f32[8,128,1024]{2,1,0:T(8,128)S(1)}, u32[]{:S(2)}) %copy-start.4) | copy-done | bytes 4194328
  132.0 0.2 all-to-all-done.2.wq_ref
  132.2 1.6 %copy-done = f32[1024,512]{1,0:T(8,128)S(1)} copy-done((f32[1024,512]{1,0:T(8,128)S(1)}, f32[1024,512]{1,0:T(8,128)}, u32[]{:S(2)}) %copy-start) | copy-done | bytes 2097176
  133.8 2.2 %copy-done.5 = f32[8,128,1024]{2,1,0:T(8,128)S(1)} copy-done((f32[8,128,1024]{2,1,0:T(8,128)S(1)}, f32[8,128,1024]{2,1,0:T(8,128)}, u32[]{:S(2)}) %copy-start.5) | copy-done | bytes 4194328
  136.0 14.9 %shard_map.44 = (f32[1024,1024]{1,0:T(8,128)}, f32[1024,512]{1,0:T(8,128)}) custom-call(s32[2]{0:T(128)S(1)} %pad_add_fusion.at_ref, s32[2,128]{1,0:T(2,128)S(1)} %copy-done.1, f32[16,1024,128]{2,1,0:T(8,128)} %bitcast.7, f32[16,256,128]{2,1,0:T(8,128)S(1)} %all-to-all-done.2.wq_ref, f32[1024,512]{1,0:T(8,128)S(1)} %copy-done, ...), custom_call_target="tpu_custom_call" | custom-call | flops 10000000000 | bytes 20000000 | tf_op jit(solution)/shard_map/pallas_call | solution.py:309
  (7 shorter events, 0.0 us)
Async XLA Ops:
  8.9 26.8 %all-to-all-start = ((f32[16,64,128]{2,1,0:T(8,128)}), f32[16,64,128]{2,1,0:T(8,128)S(1)}, u32[]{:S(2)}, u32[]{:S(2)}) async-start(f32[16,64,128]{2,1,0:T(8,128)} %bitcast.3), calls=%async_computation | async-start | bytes 1048576 | tf_op jit(solution)/shard_map/all_to_all | solution.py:371
  20.4 111.8 %all-gather.3.cloned.1.call-start = ((), (), s32[]{:S(2)}) async-start(), calls=%async_computation.3 | async-start | bytes 8912896 | tf_op jit(solution)/shard_map/all_gather | solution.py:376
  36.6 28.0 %copy-start.6 = (f32[1024,128]{1,0:T(8,128)S(1)}, f32[1024,128]{1,0:T(8,128)}, u32[]{:S(2)}) copy-start(f32[1024,128]{1,0:T(8,128)} %slice.13) | copy-start | bytes 1572868
  59.7 13.2 %collective-permute-start.2 = (f32[16,3,64,128]{3,2,1,0:T(8,128)S(1)}, f32[16,3,64,128]{3,2,1,0:T(8,128)}, u32[]{:S(2)}, u32[]{:S(2)}) collective-permute-start(f32[16,3,64,128]{3,2,1,0:T(8,128)S(1)} %all_to_all.15.own_ref), channel_id=1, source_target_pairs={{0,1},{1,0},{2,3},{3,2},{4,5},{5,4},{6,7},{7,6},{8,9},{9,8},{10,11... | collective-permute-start | bytes 4718600 | tf_op jit(solution)/shard_map/ppermute | solution.py:380
  64.5 26.3 %collective-permute-start.1 = (f32[256,128]{1,0:T(8,128)S(1)}, f32[256,128]{1,0:T(8,128)S(1)}, u32[]{:S(2)}, u32[]{:S(2)}) collective-permute-start(f32[256,128]{1,0:T(8,128)S(1)} %get-tuple-element.34), channel_id=1, source_target_pairs={{0,16},{1,48},{2,80},{3,112},{4,144},{5,176},{6,208},{7,240},{16,1... | collective-permute-start | bytes 393224 | tf_op jit(solution)/shard_map/ppermute | solution.py:384
  66.6 24.3 %collective-permute-start = (f32[256,128]{1,0:T(8,128)S(1)}, f32[256,128]{1,0:T(8,128)S(1)}, u32[]{:S(2)}, u32[]{:S(2)}) collective-permute-start(f32[256,128]{1,0:T(8,128)S(1)} %get-tuple-element.35), channel_id=1, source_target_pairs={{0,0},{1,32},{2,64},{3,96},{4,128},{5,160},{6,192},{7,224},{16,17}... | collective-permute-start | bytes 393224 | tf_op jit(solution)/shard_map/ppermute | solution.py:384
  88.9 2.0 %copy-start.2 = (f32[8,128,1024]{2,1,0:T(8,128)}, f32[8,128,1024]{2,1,0:T(8,128)S(1)}, u32[]{:S(2)}) copy-start(f32[8,128,1024]{2,1,0:T(8,128)S(1)} %get-tuple-element.28.w_in) | copy-start | bytes 12582916
  92.4 39.8 %all-to-all-start.2 = ((f32[16,256,128]{2,1,0:T(8,128)}), f32[16,256,128]{2,1,0:T(8,128)S(1)}, u32[]{:S(2)}, u32[]{:S(2)}) async-start(f32[16,256,128]{2,1,0:T(8,128)} %broadcast_in_dim.10), calls=%async_computation.2 | async-start | bytes 4194304 | tf_op jit(solution)/shard_map/all_to_all | solution.py:395
  103.1 2.2 %copy-start.3 = (f32[8,128,1024]{2,1,0:T(8,128)S(1)}, f32[8,128,1024]{2,1,0:T(8,128)}, u32[]{:S(2)}) copy-start(f32[8,128,1024]{2,1,0:T(8,128)} %copy-done.2) | copy-start | bytes 12582916
  105.3 26.9 %copy-start.1 = (s32[2,128]{1,0:T(2,128)S(1)}, s32[2,128]{1,0:T(2,128)}, u32[]{:S(2)}) copy-start(s32[2,128]{1,0:T(2,128)} %pattern_ref.1) | copy-start | bytes 3076
  130.0 2.0 %copy-start.4 = (f32[8,128,1024]{2,1,0:T(8,128)}, f32[8,128,1024]{2,1,0:T(8,128)S(1)}, u32[]{:S(2)}) copy-start(f32[8,128,1024]{2,1,0:T(8,128)S(1)} %get-tuple-element.32.work) | copy-start | bytes 12582916
  132.2 1.6 %copy-start = (f32[1024,512]{1,0:T(8,128)S(1)}, f32[1024,512]{1,0:T(8,128)}, u32[]{:S(2)}) copy-start(f32[1024,512]{1,0:T(8,128)} %m_ref.1) | copy-start | bytes 6291460
  133.8 2.2 %copy-start.5 = (f32[8,128,1024]{2,1,0:T(8,128)S(1)}, f32[8,128,1024]{2,1,0:T(8,128)}, u32[]{:S(2)}) copy-start(f32[8,128,1024]{2,1,0:T(8,128)} %copy-done.4) | copy-start | bytes 12582916
Sparse Core Ops, SparseCore 0:
  35.8 70.0 all-gather.2
